TPU v7x, 256 devices: a whole 4x4x8 slice. The times are simulated.
256 devices in a mesh: dp: 16 (over y_lo, x, core), fsdp: 16 (over y_hi, z).
Axes of the slice: x: 4, y: 4 (y_hi: 2, y_lo: 2; y = y_hi * 2 + y_lo), z: 8, core: 2. Of those that a mesh axis runs over, the one named last changes fastest.
Arguments:
- inputs: bfloat16 [98304, 3584], P(('dp', 'fsdp')), may hold values from -7 to 7
- queries: bfloat16 [98304, 1792], P(('dp', 'fsdp')), may hold values from -14 to 14
- out_grad: bfloat16 [98304, 1792], P(('dp', 'fsdp')), may hold values from -6 to 6
- kv_weight: bfloat16 [3584, 512], P('fsdp'), may hold values from -0.09375 to 0.09375
- passage_blocks: int32 [256, 6], P(('dp', 'fsdp')), may hold values from 0 to 5, as said below
- handover: int32 [256, 6], P(('dp', 'fsdp')), may hold values from 0 to 1, as said below
Outputs:
- grad_input: bfloat16 [98304, 3584], P(('dp', 'fsdp'))
- grad_query: bfloat16 [98304, 1792], P(('dp', 'fsdp'))
- grad_weight: float32 [3584, 512], P('fsdp')
Inputs may be any that keep to these rules, and one draw needn't show every extreme that they name: `passage_blocks`: each row starts at 0 and rises by 0 or 1 from block to block; a passage's blocks all carry the same handover flag. `handover`: partners hand over the same number of blocks, at least one and at most 5.
All inputs are finite; a program needn't handle non-finite values.
Results may differ from a plain program's by a relative error of at most 0.013.
The roundings to bfloat16 on the way count: a program that leaves them out, or rounds other values in their place, can miss the bound.
Values may be sent and summed in bfloat16 or wider, within the bound.
A program may use at most 128 MiB of HBM per device.

v0:
```python
import jax
import jax.numpy as jnp
from jax import lax
from jax.sharding import PartitionSpec as P

KVH = 2
GROUP = 7
HD = 128
QH = 14


rope_base = 1000000.0


def from_partner(block, axis, bit):
    count = lax.axis_size(axis)
    route = []
    for low in range(count):
        high = low | 1 << bit
        if high != low and high < count:
            route += [(low, high), (high, low)]
    return lax.ppermute(block, axis, route)


def block_offsets(ids, block_rows):
    count = ids.shape[0]
    order = jnp.arange(count, dtype=jnp.int32)
    same = ids[:, None] == ids[None, :]
    first = jnp.min(jnp.where(same, order[None, :], count), axis=1)
    return (order - first) * block_rows


def expand_rows(values, block_rows):
    inner = jnp.zeros((block_rows,), jnp.int32)
    return (values[:, None] + inner[None, :]).reshape(-1)


def row_positions(offsets, block_rows):
    inner = jnp.arange(block_rows, dtype=jnp.int32)
    return (offsets[:, None] + inner[None, :]).reshape(-1)


def rotary(positions):
    half = HD // 2
    freq = rope_base ** (-(jnp.arange(half, dtype=jnp.float32) * 2.0) / HD)
    angle = positions.astype(jnp.float32)[:, None] * freq[None, :]
    cosine = jnp.concatenate([jnp.cos(angle), jnp.cos(angle)], axis=1)
    sine = jnp.concatenate([jnp.sin(angle), jnp.sin(angle)], axis=1)
    return (cosine[:, None, :], sine[:, None, :])


def rotate(values, cosine, sine):
    half = HD // 2
    turned = jnp.concatenate([-values[..., half:], values[..., :half]], axis=-1)
    return values * cosine + turned * sine


def unrotate(grads, cosine, sine):
    half = HD // 2
    scaled = grads * sine
    turned = jnp.concatenate([scaled[..., half:], -scaled[..., :half]], axis=-1)
    return grads * cosine + turned


def attend(queries, keys, values, out_grad, labels):
    rows = queries.shape[0]
    scale = 1.0 / HD**0.5
    q_heads = queries.reshape(rows, KVH, GROUP, HD)
    k_heads = keys.reshape(rows, KVH, HD)
    v_heads = values.reshape(rows, KVH, HD)
    g_heads = out_grad.reshape(rows, KVH, GROUP, HD)
    scores = (
        jnp.einsum("qghd,kgd->ghqk", q_heads, k_heads, preferred_element_type=jnp.float32) * scale
    )
    same = labels[:, None] == labels[None, :]
    scores = jnp.where(same[None, None], scores, -jnp.inf)
    top = jnp.max(scores, axis=-1, keepdims=True)
    weights = jnp.exp(scores - top)
    probs = weights / jnp.sum(weights, axis=-1, keepdims=True)
    probs_b = probs.astype(jnp.bfloat16)
    attended = jnp.einsum("ghqk,kgd->qghd", probs_b, v_heads, preferred_element_type=jnp.float32)
    delta = jnp.sum(g_heads.astype(jnp.float32) * attended, axis=-1)
    dprobs = jnp.einsum("qghd,kgd->ghqk", g_heads, v_heads, preferred_element_type=jnp.float32)
    dscores = probs * (dprobs - jnp.transpose(delta, (1, 2, 0))[..., None])
    dscores_b = dscores.astype(jnp.bfloat16)
    query_grad = (
        jnp.einsum("ghqk,kgd->qghd", dscores_b, k_heads, preferred_element_type=jnp.float32) * scale
    ).astype(jnp.bfloat16)
    key_grad = (
        jnp.einsum("ghqk,qghd->kgd", dscores_b, q_heads, preferred_element_type=jnp.float32) * scale
    )
    value_grad = jnp.einsum("ghqk,qghd->kgd", probs_b, g_heads, preferred_element_type=jnp.float32)
    return (query_grad.reshape(rows, QH * HD), key_grad, value_grad)


def project_rows(inputs, weight):
    return jnp.dot(inputs, weight, preferred_element_type=jnp.float32)


def project_back(kv_grad, weight):
    return jnp.einsum("rk,ck->rc", kv_grad, weight, preferred_element_type=jnp.float32)


def local_grads(inputs, queries, out_grad, labels, positions, weight):
    rows = inputs.shape[0]
    projected = project_rows(inputs, weight)
    cosine, sine = rotary(positions)
    raw_keys = projected[:, : KVH * HD].reshape(rows, KVH, HD)
    keys = rotate(raw_keys, cosine, sine).astype(jnp.bfloat16).reshape(rows, KVH * HD)
    values = projected[:, KVH * HD :].astype(jnp.bfloat16)
    query_grad, key_grad, value_grad = attend(queries, keys, values, out_grad, labels)
    raw_key_grad = unrotate(key_grad, cosine, sine)
    kv_grad = jnp.concatenate(
        [raw_key_grad.reshape(rows, KVH * HD), value_grad.reshape(rows, KVH * HD)], axis=1
    ).astype(jnp.bfloat16)
    input_grad = project_back(kv_grad, weight).astype(jnp.bfloat16)
    return (input_grad, query_grad, kv_grad)


def relocate(own, other, mine, select):
    blocks = mine.shape[0]
    width = own.shape[1]
    own_blocks = own.reshape(blocks, -1, width)
    other_blocks = other.reshape(blocks, -1, width)
    taken = jnp.einsum(
        "bc,crw->brw", select.astype(own.dtype), other_blocks, preferred_element_type=jnp.float32
    ).astype(own.dtype)
    keep = (mine == 0)[:, None, None]
    return jnp.where(keep, own_blocks, taken).reshape(own.shape)


def shards(inputs, queries, out_grad, kv_weight, passage_blocks, handover):
    rows = inputs.shape[0]
    blocks = passage_blocks.shape[1]
    block_rows = rows // blocks
    half_bit = lax.axis_size("dp").bit_length() - 2
    partner_info = from_partner(jnp.concatenate([handover, passage_blocks], axis=0), "dp", half_bit)
    mine = handover[0]
    theirs = partner_info[0]
    own_ids = passage_blocks[0]
    rank_mine = jnp.cumsum(mine) - 1
    rank_theirs = jnp.cumsum(theirs) - 1
    select = (
        (mine[:, None] == 1) & (theirs[None, :] == 1) & (rank_mine[:, None] == rank_theirs[None, :])
    )
    weight = lax.all_gather(kv_weight, "fsdp", axis=0, tiled=True)
    own_offsets = block_offsets(own_ids, block_rows)
    labels = expand_rows(own_ids, block_rows)
    positions = row_positions(own_offsets, block_rows)
    input_grad, query_grad, kv_grad = local_grads(
        inputs, queries, out_grad, labels, positions, weight
    )
    moved = from_partner((input_grad, query_grad), "dp", half_bit)
    grad_input = relocate(input_grad, moved[0], mine, select)
    grad_query = relocate(query_grad, moved[1], mine, select)
    share = lax.psum_scatter(
        jnp.einsum("rc,rk->ck", inputs, kv_grad, preferred_element_type=jnp.float32),
        "fsdp",
        scatter_dimension=0,
        tiled=True,
    )
    grad_weight = lax.psum(share, "dp")
    return (grad_input, grad_query, grad_weight)


def solution(mesh):
    placed = (
        P(("dp", "fsdp"), None),
        P(("dp", "fsdp"), None),
        P(("dp", "fsdp"), None),
        P("fsdp", None),
        P(("dp", "fsdp"), None),
        P(("dp", "fsdp"), None),
    )
    return jax.shard_map(
        shards,
        mesh=mesh,
        in_specs=placed,
        out_specs=(P(("dp", "fsdp"), None), P(("dp", "fsdp"), None), P("fsdp", None)),
        check_vma=False,
    )
```

profile of v0, /device:TPU:1, one launch (start us, length us, event | category | flops | bytes accessed | tf_op | source)
XLA Modules:
  0.0 521.1 jit_solution(6367246474276333780)
XLA Ops:
  8.0 0.9 select_reduce_fusion
  9.8 2.5 copy.76
  12.3 2.5 copy.79
  15.3 0.9 broadcast_multiply_fusion
  17.0 90.6 %all-gather.2.cloned.1.call-done = bf16[3584,512]{1,0:T(8,128)(2,1)} async-done(((bf16[224,512]{1,0:T(8,128)(2,1)}), bf16[3584,512]{1,0:T(8,128)(2,1)}) %all-gather.2.cloned.1.call-update) | async-done | bytes 3670032 | tf_op jit(solution)/shard_map/all_gather | solution.py:146
  107.6 3.6 fusion.36
  112.1 1.0 reshape.182
  113.3 1.1 fusion.19
  114.4 7.2 %fusion.35 = (f32[2,7,384]{2,1,0:T(8,128)S(1)}, f32[2,7,384,384]{2,3,1,0:T(8,128)}) fusion(pred[384,384]{0,1:T(8,128)(4,1)} %broadcast_compare_fusion, bf16[384,2,128,1]{0,2,3,1:T(8,128)(2,1)S(1)} %fusion.19, bf16[384,2,7,128]{0,3,2,1:T(8,128)(2,1)} %bitcast.103), kind=kOutput, calls=%fused_computation.72 | convolution fusion | flops 536740224 | bytes 9999360 | tf_op jit(solution)/shard_map/sub | solution.py:78
  121.6 4.3 fusion.9
  125.9 1.3 fusion.13
  127.2 1.0 fusion.11
  128.2 1.1 copy-done.5
  129.3 1.6 fusion.2
  130.9 1.3 convolution_bitcast_fusion.2
  133.7 5.1 convolution_bitcast_fusion
  138.7 8.4 %copy.114 = f32[3584,512]{1,0:T(8,128)} copy(f32[3584,512]{0,1:T(8,128)} %convolution_bitcast_fusion) | data formatting | bytes 14680064
  148.1 5.4 %convolution_convert_fusion.1 = bf16[384,3584]{1,0:T(8,128)(2,1)} fusion(bf16[3584,512]{1,0:T(8,128)(2,1)} %all-gather.2.cloned.1.call-done, bf16[384,256]{0,1:T(8,128)(2,1)S(1)} %bitcast.110, bf16[384,256]{0,1:T(8,128)(2,1)S(1)} %bitcast.113), kind=kOutput, calls=%fused_computation.9 | convolution fusion | flops 1411448832 | bytes 6815744 | tf_op jit(solution)/shard_map/rk,ck->rc/dot_general | solution.py:101
  153.7 1.0 multiply_convert_fusion
  154.7 0.9 copy.91
  155.6 1.2 collective-permute-start.2
  157.4 102.2 %collective-permute-done = s32[2,6]{1,0:T(2,128)S(1)} collective-permute-done((s32[2,6]{1,0:T(2,128)S(1)}, s32[2,6]{1,0:T(2,128)S(1)}, u32[]{:S(2)}, u32[]{:S(2)}) %collective-permute-start) | collective-permute-done | bytes 80 | tf_op jit(solution)/shard_map/ppermute | solution.py:22
  259.8 2.0 copy.90
  261.8 4.0 reshape_reshape.3
  265.7 3.4 fusion.10
  269.1 1.3 copy.94
  270.4 114.7 %reduce-scatter.4.cloned.1.call-done = f32[224,512]{1,0:T(8,128)} async-done(((f32[3584,512]{1,0:T(8,128)}), f32[224,512]{1,0:T(8,128)}) %reduce-scatter.4.cloned.1.call-update) | async-done | bytes 458768
  385.1 2.0 copy.115
  387.1 8.5 %fusion.4 = bf16[6,64,3584]{2,0,1:T(8,128)(2,1)S(1)} fusion(bf16[6,64,3584]{2,1,0:T(8,128)(2,1)} %bitcast.20, bf16[6,64,3584]{2,1,0:T(8,128)(2,1)} %bitcast.28, pred[6]{0:T(512)(128)(4,1)S(1)} %get-tuple-element.26, s32[6]{0:T(128)S(1)} %add_bitcast_fusion, s32[6]{0:T(128)S(1)} %add_bitcast_fusion.1, pred[6]{0:T(512)(128)(4,1)S(1)} %compare_bitcast_fusion, ...), kind=kOutput, calls=%fused_computation.10 | convolution fusion | flops 19267692 | bytes 8257602 | tf_op jit(solution)/shard_map/bc,crw->brw/dot_general | solution.py:125
  395.6 2.3 copy.88
  397.9 114.6 %all-reduce.2.cloned.1.call-done = f32[224,512]{0,1:T(8,128)} async-done(((f32[224,512]{0,1:T(8,128)}), f32[224,512]{0,1:T(8,128)}) %all-reduce.2.cloned.1.call-update) | async-done | bytes 458768 | tf_op jit(solution)/shard_map/psum | solution.py:162
  512.6 2.0 copy.95
  (59 shorter events, 7.6 us)
Async XLA Ops:
  7.2 100.5 %copy-start = (bf16[384,3584]{1,0:T(8,128)(2,1)S(1)}, bf16[384,3584]{1,0:T(8,128)(2,1)}, u32[]{:S(2)}) copy-start(bf16[384,3584]{1,0:T(8,128)(2,1)} %param.6) | copy-start | bytes 8257540
  7.2 100.4 %all-gather.2.cloned.1.call-start = ((), (), s32[]{:S(2)}) async-start(), calls=%async_computation.1 | async-start | bytes 3899392 | tf_op jit(solution)/shard_map/all_gather | solution.py:146
  7.9 377.1 %reduce-scatter.4.cloned.1.call-start = ((), (), s32[]{:S(2)}) async-start(), calls=%async_computation.3 | async-start | bytes 7798784
  121.6 4.3 copy-start.4
  125.9 3.3 copy-start.5
  129.3 1.6 copy-start.6
  130.9 1.9 copy-start.2
  130.9 1.9 copy-start.8
  130.9 2.0 copy-start.7
  133.0 0.7 copy-start.9
  147.1 0.9 copy-start.10
  147.2 365.4 %all-reduce.2.cloned.1.call-start = ((), (), s32[]{:S(2)}) async-start(), calls=%async_computation.2 | async-start | bytes 1048576 | tf_op jit(solution)/shard_map/psum | solution.py:162
  148.1 5.7 %copy-start.3 = (bf16[2,7,384,384]{2,3,1,0:T(8,128)(2,1)S(1)}, bf16[2,7,384,384]{2,3,1,0:T(8,128)(2,1)}, u32[]{:S(2)}) copy-start(bf16[2,7,384,384]{2,3,1,0:T(8,128)(2,1)} %copy-done.2) | copy-start | bytes 12386308
  153.4 233.7 %collective-permute-start.1 = (bf16[384,3584]{1,0:T(8,128)(2,1)}, bf16[384,3584]{1,0:T(8,128)(2,1)}, u32[]{:S(2)}, u32[]{:S(2)}) collective-permute-start(bf16[384,3584]{1,0:T(8,128)(2,1)} %convolution_convert_fusion.1), channel_id=1, source_target_pairs={{0,128},{128,0},{16,144},{144,16},{32,160},{160,32},{48,176},{176,... | collective-permute-start | bytes 8257544 | tf_op jit(solution)/shard_map/ppermute | solution.py:22
  154.7 2.1 copy-start.11
  154.7 2.1 copy-start.12
  155.6 110.1 %collective-permute-start.2 = (bf16[384,1792]{1,0:T(8,128)(2,1)S(1)}, bf16[384,1792]{1,0:T(8,128)(2,1)}, u32[]{:S(2)}, u32[]{:S(2)}) collective-permute-start(bf16[384,1792]{1,0:T(8,128)(2,1)S(1)} %copy.91), channel_id=1, source_target_pairs={{0,128},{128,0},{16,144},{144,16},{32,160},{160,32},{48,176},{176,... | collective-permute-start | bytes 4128776 | tf_op jit(solution)/shard_map/ppermute | solution.py:22
  156.8 102.7 %collective-permute-start = (s32[2,6]{1,0:T(2,128)S(1)}, s32[2,6]{1,0:T(2,128)S(1)}, u32[]{:S(2)}, u32[]{:S(2)}) collective-permute-start(s32[2,6]{1,0:T(2,128)S(1)} %pad_add_fusion), channel_id=1, source_target_pairs={{0,128},{128,0},{16,144},{144,16},{32,160},{160,32},{48,176},{176,... | collective-permute-start | bytes 152 | tf_op jit(solution)/shard_map/ppermute | solution.py:22
  387.1 127.4 %copy-start.1 = (bf16[384,3584]{1,0:T(8,128)(2,1)S(1)}, bf16[384,3584]{1,0:T(8,128)(2,1)}, u32[]{:S(2)}) copy-start(bf16[384,3584]{1,0:T(8,128)(2,1)} %param.6) | copy-start | bytes 8257540
Sparse Core Ops, SparseCore 0:
  10.6 96.9 all-gather.1
  147.3 237.7 reduce-scatter.3
  387.9 124.6 all-reduce.1
where the time goes:
time: 522 us; the launch traced here: 521 us
  waiting for transfers between devices  423 us (81%)
  matrix products  39.1 us (7%)
  local copies, waits for them, and re-layouts  33.9 us (6%)
  between operations  14 us (3%)
  other arithmetic  9.06 us (2%)
    unnamed x4, waiting for transfers between devices  115 us
    psum x1, waiting for transfers between devices, shards(): grad_weight = lax.psum(share, 'dp')  115 us
    ppermute x3, waiting for transfers between devices, from_partner(): return lax.ppermute(block, axis, route)  102 us
    all_gather x1, waiting for transfers between devices, shards(): weight = lax.all_gather(kv_weight, 'fsdp', axis=0, tiled=True)  90.6 us
    unnamed x31, local copies, waits for them, and re-layouts  20.5 us
    dot_general x2, matrix products, relocate(): jnp.einsum('bc,crw->brw', select.astype(own.dtype), other_blocks, preferr...  11.8 us
  transfers between devices with their start and end apart: 6, of which 4 were waited for; matrix products, arithmetic and copies ran while one was open for 8% of the time, Pallas kernels for 0%

commit v1 on v0

v1 whole, which is shorter than its diff:
```python
import functools

import jax
import jax.numpy as jnp
import numpy as np
from jax import lax
from jax.experimental import pallas as pl
from jax.experimental.pallas import tpu as pltpu
from jax.sharding import PartitionSpec as P

KVH = 2
GROUP = 7
HD = 128
QH = 14
NB = 6
BLK = 64
SENT = NB - 1
ROWS = NB * BLK
D = 3584
NX, NZ, NF = 4, 8, 16
SHARD = D // NF
HALF = SHARD // 2
KV = 2 * KVH * HD
ROPE_BASE = 1000000.0
MESH = pl.DeviceIdType.MESH
VMEM = pl.BlockSpec(memory_space=pltpu.VMEM)
LIMIT = 50 * 1024 * 1024
f32, bf16 = jnp.float32, jnp.bfloat16


def place():
    d, f = lax.axis_index("dp"), lax.axis_index("fsdp")
    return d // 8, (d // 2) % NX, d % 2, f // NZ, f % NZ


def device(lo, x, c, hi, z):
    return (lo * 8 + x * 2 + c, hi * NZ + z)


def greet(peers):
    barrier = pltpu.get_barrier_semaphore()
    for peer in peers:
        pl.semaphore_signal(barrier, inc=1, device_id=peer, device_id_type=MESH)
    pl.semaphore_wait(barrier, len(peers))


def columns(index, width=HD):
    return pl.ds(pl.multiple_of(index * width, width), width)


HOPS = {(0, 1): 4, (0, -1): 3, (1, 1): 3, (1, -1): 4}
RINGS = list(HOPS)


def gather_kernel(w_ref, out_ref, send, ring_recv, x_recv, own_recv, far_recv, y_recv):
    lo, x, c, hi, z = place()
    right_z, left_z = (z + 1) % NZ, (z + NZ - 1) % NZ
    z_peer = {1: device(lo, x, c, hi, right_z), -1: device(lo, x, c, hi, left_z)}
    x_peer = {1: device(lo, (x + 1) % NX, c, hi, z), -1: device(lo, (x + NX - 1) % NX, c, hi, z)}
    y_peer = device(1 - lo, x, c, 1 - hi, z)
    sibling = device(lo, x, 1 - c, hi, z)
    greet([z_peer[1], z_peer[-1], x_peer[1], x_peer[-1], y_peer, sibling])
    out_ref[hi, z] = w_ref[...]
    near = columns(2 * (x % 2) + c)
    far = columns(2 * (1 - x % 2) + c)
    side = (hi, 1 - hi)
    started = []

    def push(part, peer, recv):
        copy = pltpu.make_async_remote_copy(
            src_ref=part,
            dst_ref=part,
            send_sem=send.at[len(started)],
            recv_sem=recv,
            device_id=peer,
            device_id_type=MESH,
        )
        copy.start()
        started.append(copy)

    def arrived(part, recv):
        pltpu.make_async_remote_copy(
            src_ref=part,
            dst_ref=part,
            send_sem=send.at[0],
            recv_sem=recv,
            device_id=sibling,
            device_id_type=MESH,
        ).wait_recv()

    def piece(ring, way, hop, cols):
        source = (z + NZ - way * hop) % NZ
        return out_ref.at[side[ring], source, :, cols]

    def slot(ring, way, hop):
        return RINGS.index((ring, way)) * 4 + hop

    push(out_ref.at[hi, z], y_peer, y_recv.at[0])
    for way in (1, -1):
        push(piece(0, way, 0, near), z_peer[way], ring_recv.at[slot(0, way, 0)])
    arrived(out_ref.at[1 - hi, z], y_recv.at[0])
    for way in (-1, 1):
        push(piece(1, way, 0, near), z_peer[way], ring_recv.at[slot(1, way, 0)])

    def across(ring, way, hop):
        part = piece(ring, way, hop, far)
        arrived(part, x_recv.at[slot(ring, way, hop - 1)])
        push(part, sibling, far_recv.at[slot(ring, way, hop - 1)])

    late = []
    for hop in range(1, 5):
        for ring, way in RINGS:
            if hop > HOPS[ring, way]:
                continue
            part = piece(ring, way, hop, near)
            at = slot(ring, way, hop - 1)
            arrived(part, ring_recv.at[at])
            if hop < HOPS[ring, way]:
                push(part, z_peer[way], ring_recv.at[at + 1])
            push(part, x_peer[way], x_recv.at[at])
            push(part, sibling, own_recv.at[at])
            late.append((ring, way, hop))
            if len(late) > 3:
                across(*late.pop(0))
    for item in late:
        across(*item)
    for ring, way in RINGS:
        for hop in range(1, HOPS[ring, way] + 1):
            at = slot(ring, way, hop - 1)
            arrived(piece(ring, way, hop, columns(2 * (x % 2) + 1 - c)), own_recv.at[at])
            arrived(piece(ring, way, hop, columns(2 * (1 - x % 2) + 1 - c)), far_recv.at[at])
    for copy in started:
        copy.wait_send()


def gather_weight(weight):
    dma = pltpu.SemaphoreType.DMA
    out = pl.pallas_call(
        gather_kernel,
        name="gather_weight",
        out_shape=jax.ShapeDtypeStruct((2, NZ, SHARD, KV), bf16),
        in_specs=[VMEM],
        out_specs=VMEM,
        scratch_shapes=[dma((64,)), dma((16,)), dma((16,)), dma((16,)), dma((16,)), dma((1,))],
        compiler_params=pltpu.CompilerParams(
            collective_id=0, has_side_effects=True, vmem_limit_bytes=LIMIT
        ),
    )(weight)
    return out.reshape(D, KV)


def handed_blocks(flags):
    rank, ranks = jnp.int32(0), []
    for b in range(NB):
        ranks.append(rank)
        rank = rank + flags[b]
    picks = []
    for r in range(SENT):
        pick = jnp.int32(0)
        for b in range(NB):
            pick = jnp.where((flags[b] == 1) & (ranks[b] == r), b, pick)
        picks.append(pick)
    return ranks, picks


def dot(a, b, dims):
    return lax.dot_general(a, b, ((dims[:1], dims[1:]), ((), ())), preferred_element_type=f32)


def attend_kernel(
    ids_ref, flags_ref, x_ref, w_ref, freq_ref, q_ref, g_ref,
    qg_ref, qp_ref, kvg_ref, kvp_ref,
    keys, keys_t, vals, kacc, vacc, bias, cosine, sine,
):
    h = pl.program_id(0)
    group = h // GROUP
    member = h % GROUP
    scale = 1.0 / HD**0.5
    picks = handed_blocks([flags_ref[0, b] for b in range(NB)])[1]

    @pl.when(h == 0)
    def _():
        ids = [ids_ref[0, b] for b in range(NB)]
        first = [jnp.int32(0)]
        for b in range(1, NB):
            first.append(jnp.where(ids[b] == ids[b - 1], first[b - 1], b * BLK))
        row = lax.broadcasted_iota(jnp.int32, (ROWS, HD), 0)
        tall = lax.broadcasted_iota(jnp.int32, (ROWS, ROWS), 0)
        wide = lax.broadcasted_iota(jnp.int32, (ROWS, ROWS), 1)
        start = jnp.zeros((ROWS, HD), jnp.int32)
        label_k = jnp.zeros((ROWS, ROWS), jnp.int32)
        label_q = jnp.zeros((ROWS, ROWS), jnp.int32)
        for b in range(NB):
            start = jnp.where(row >= b * BLK, first[b], start)
            label_k = jnp.where(tall >= b * BLK, ids[b], label_k)
            label_q = jnp.where(wide >= b * BLK, ids[b], label_q)
        bias[...] = jnp.where(label_k == label_q, 0.0, -jnp.inf)
        angle = (row - start).astype(f32) * freq_ref[...]
        cosine[...] = jnp.cos(angle)
        lane = lax.broadcasted_iota(jnp.int32, (ROWS, HD), 1)
        turn = jnp.sin(angle)
        sine[...] = jnp.where(lane < HD // 2, -turn, turn)
        projected = dot(x_ref[...], w_ref[...], (1, 0))
        for g in range(KVH):
            raw = projected[:, g * HD : (g + 1) * HD]
            key = raw * cosine[...] + pltpu.roll(raw, HD // 2, 1) * sine[...]
            keys[g] = key.astype(bf16)
            keys_t[g] = key.T.astype(bf16)
            vals[g] = projected[:, (KVH + g) * HD : (KVH + g + 1) * HD].astype(bf16)

    @pl.when(member == 0)
    def _():
        kacc[...] = jnp.zeros_like(kacc)
        vacc[...] = jnp.zeros_like(vacc)

    query, grad = q_ref[...], g_ref[...]
    scores = dot(keys[group], query, (1, 1)) * scale + bias[...]
    weights = jnp.exp(scores - jnp.max(scores, axis=0, keepdims=True))
    probs = weights * (1.0 / jnp.sum(weights, axis=0, keepdims=True))
    probs_b = probs.astype(bf16)
    dprobs = dot(vals[group], grad, (1, 1))
    delta = jnp.sum(probs_b.astype(f32) * dprobs, axis=0, keepdims=True)
    dscores_b = (probs * (dprobs - delta)).astype(bf16)
    vacc[...] += dot(probs_b, grad, (1, 0))
    kacc[...] += dot(dscores_b, query, (1, 0))
    query_grad = dot(keys_t[group], dscores_b, (1, 0)) * scale
    qg_ref[...] = query_grad.T.astype(bf16)
    for r in range(SENT):
        at = pl.ds(pl.multiple_of(picks[r] * BLK, BLK), BLK)
        qp_ref[r * BLK : (r + 1) * BLK, :] = qg_ref[at, :]

    @pl.when(member == GROUP - 1)
    def _():
        grad_k = kacc[...] * scale
        raw = grad_k * cosine[...] - pltpu.roll(grad_k, HD // 2, 1) * sine[...]
        kvg_ref[:, columns(group)] = raw.astype(bf16)
        kvg_ref[:, columns(KVH + group)] = vacc[...].astype(bf16)

    @pl.when(h == QH - 1)
    def _():
        for r in range(SENT):
            at = pl.ds(pl.multiple_of(picks[r] * BLK, BLK), BLK)
            kvp_ref[r * BLK : (r + 1) * BLK, :] = kvg_ref[at, :]


def whole(*shape):
    return pl.BlockSpec(shape, lambda *_: (0,) * len(shape))


def attend(inputs, queries, out_grad, weight, ids, flags):
    freq = ROPE_BASE ** (-(np.arange(HD // 2, dtype=np.float32) * 2.0) / HD)
    freq = jnp.asarray(np.concatenate([freq, freq])[None, :].astype(np.float32))
    head = pl.BlockSpec((ROWS, HD), lambda h, *_: (0, h))
    packed = pl.BlockSpec((SENT * BLK, HD), lambda h, *_: (0, h))
    return pl.pallas_call(
        attend_kernel,
        name="attention_backward",
        out_shape=(
            jax.ShapeDtypeStruct((ROWS, QH * HD), bf16),
            jax.ShapeDtypeStruct((SENT * BLK, QH * HD), bf16),
            jax.ShapeDtypeStruct((ROWS, KV), bf16),
            jax.ShapeDtypeStruct((SENT * BLK, KV), bf16),
        ),
        grid_spec=pltpu.PrefetchScalarGridSpec(
            num_scalar_prefetch=2,
            grid=(QH,),
            in_specs=[whole(ROWS, D), whole(D, KV), whole(1, HD), head, head],
            out_specs=(head, packed, whole(ROWS, KV), whole(SENT * BLK, KV)),
            scratch_shapes=[
                pltpu.VMEM((KVH, ROWS, HD), bf16),
                pltpu.VMEM((KVH, HD, ROWS), bf16),
                pltpu.VMEM((KVH, ROWS, HD), bf16),
                pltpu.VMEM((ROWS, HD), f32),
                pltpu.VMEM((ROWS, HD), f32),
                pltpu.VMEM((ROWS, ROWS), f32),
                pltpu.VMEM((ROWS, HD), f32),
                pltpu.VMEM((ROWS, HD), f32),
            ],
        ),
        compiler_params=pltpu.CompilerParams(vmem_limit_bytes=LIMIT),
    )(ids, flags, inputs, weight, freq, queries, out_grad)


CH = 4
PER = NF // CH


def exchange_kernel(
    x_ref, kvg_ref, qp_ref, kvp_ref,
    qr_ref, kvr_ref, gw_ref,
    part, sib, tot, relay_in, relay_out, direct, summed, after_x, z_in, after_z, y_in, final,
    send, swap_recv, sib_recv, relay_recv, direct_recv, summed_recv, z_recv, y_recv, share_recv,
):
    lo, x, c, hi, z = place()
    y = 2 * hi + lo
    sibling = device(lo, x, 1 - c, hi, z)
    partner = device(1 - lo, x, c, hi, z)
    cross = device(1 - lo, x, c, 1 - hi, z)
    across = device(lo, x, c, 1 - hi, z)
    xp, xm, xo = (x + 1) % NX, (x + NX - 1) % NX, (x + 2) % NX
    x_side = (xp, xm)
    x_peer = [device(lo, xs, c, hi, z) for xs in x_side]
    z_peer = [device(lo, x, c, hi, (z + s) % NZ) for s in range(1, NZ)]
    row_peer = [
        device(lo, (x + dx) % NX, (c + dc) % 2, hi, z)
        for dx in range(NX)
        for dc in range(2)
        if dx or dc
    ]
    greet(row_peer + z_peer + [partner, cross, across])
    started = []

    def push(src, dst, peer, recv):
        copy = pltpu.make_async_remote_copy(
            src_ref=src,
            dst_ref=dst,
            send_sem=send.at[len(started)],
            recv_sem=recv,
            device_id=peer,
            device_id_type=MESH,
        )
        copy.start()
        started.append(copy)

    def arrived(dst, recv):
        pltpu.make_async_remote_copy(
            src_ref=dst,
            dst_ref=dst,
            send_sem=send.at[0],
            recv_sem=recv,
            device_id=sibling,
            device_id_type=MESH,
        ).wait_recv()

    push(kvp_ref, kvr_ref, partner, swap_recv.at[0])
    push(qp_ref, qr_ref, partner, swap_recv.at[1])

    def owners(k):
        return pl.ds(k * PER, PER)

    def sub(k, side):
        return pl.ds(k * PER + 2 * side, 2)

    def box(xs):
        return pl.ds(pl.multiple_of((xs // 2) * HALF, HALF), HALF), columns(xs % 2)

    def chunk_sum(k):
        arrived(sib.at[owners(k)], sib_recv.at[k])
        own = part[owners(k), :, columns(c, 2 * HD)].astype(f32)
        tot[owners(k)] = (own + sib[owners(k)].astype(f32)).astype(bf16)
        far_rows, far_cols = box(xo)
        for side in range(2):
            at = 2 * k + side
            push(
                tot.at[sub(k, side), far_rows, far_cols],
                relay_in.at[at],
                x_peer[side],
                relay_recv.at[at],
            )
        for side in range(2):
            rows, cols = box(x_side[side])
            at = 2 * k + side
            push(tot.at[sub(k, 1 - side), rows, cols], direct.at[at], x_peer[side], direct_recv.at[at])

    def relay(k):
        for side in range(2):
            at = 2 * k + side
            rows, cols = box(x_side[side])
            arrived(relay_in.at[at], relay_recv.at[at])
            mine = tot[sub(k, side), rows, cols].astype(f32)
            relay_out[at] = (mine + relay_in[at].astype(f32)).astype(bf16)
            push(relay_out.at[at], summed.at[at], x_peer[side], summed_recv.at[at])

    def x_total(k):
        rows, cols = box(x)
        for side in range(2):
            at, other = 2 * k + side, 2 * k + 1 - side
            arrived(direct.at[other], direct_recv.at[other])
            arrived(summed.at[at], summed_recv.at[at])
            mine = tot[sub(k, side), rows, cols].astype(f32)
            got = summed[at].astype(f32) + direct[other].astype(f32)
            after_x[sub(k, side)] = (mine + got).astype(bf16)

    for k in range(CH):
        wide = SHARD * PER
        product = dot(x_ref[:, k * wide : (k + 1) * wide], kvg_ref[...], (0, 0))
        part[owners(k)] = product.astype(bf16).reshape(PER, SHARD, KV)
        push(
            part.at[owners(k), :, columns(1 - c, 2 * HD)],
            sib.at[owners(k)],
            sibling,
            sib_recv.at[k],
        )
        if k:
            chunk_sum(k - 1)
    chunk_sum(CH - 1)
    for k in range(CH):
        relay(k)
    for side in range(2):
        for k in (2 * side, 2 * side + 1):
            x_total(k)
        for s in range(1, NZ):
            at = side * (NZ - 1) + s - 1
            push(after_x.at[side * NZ + (z + s) % NZ], z_in.at[at], z_peer[s - 1], z_recv.at[at])
    for side in range(2):
        total = after_x[side * NZ + z].astype(f32)
        for s in range(1, NZ):
            at = side * (NZ - 1) + s - 1
            arrived(z_in.at[at], z_recv.at[at])
            total = total + z_in[at].astype(f32)
        after_z[side] = total.astype(bf16)
    y_in[y] = after_z[hi]
    push(after_z.at[hi], y_in.at[y], partner, y_recv.at[0])
    push(after_z.at[1 - hi], y_in.at[y], cross, y_recv.at[1])
    push(after_z.at[1 - hi], y_in.at[y], across, y_recv.at[2])
    arrived(y_in.at[2 * hi + 1 - lo], y_recv.at[0])
    arrived(y_in.at[2 * (1 - hi) + 1 - lo], y_recv.at[1])
    arrived(y_in.at[2 * (1 - hi) + lo], y_recv.at[2])
    total = y_in[0].astype(f32)
    for at in range(1, 4):
        total = total + y_in[at].astype(f32)
    final[...] = total.astype(bf16)

    def place_of(xs, cs):
        return gw_ref.at[
            pl.ds(pl.multiple_of((xs // 2) * HALF, HALF), HALF), columns(2 * cs + xs % 2)
        ]

    at = 0
    for dx in range(NX):
        for dc in range(2):
            if dx or dc:
                push(final, place_of(x, c), row_peer[at], share_recv.at[at])
                at += 1
    gw_ref[pl.ds(pl.multiple_of((x // 2) * HALF, HALF), HALF), columns(2 * c + x % 2)] = final[...]
    at = 0
    for dx in range(NX):
        for dc in range(2):
            if dx or dc:
                arrived(place_of((x + NX - dx) % NX, (c + dc) % 2), share_recv.at[at])
                at += 1
    arrived(kvr_ref, swap_recv.at[0])
    arrived(qr_ref, swap_recv.at[1])
    for copy in started:
        copy.wait_send()


def exchange(inputs, kv_grad, query_pack, kv_pack):
    dma = pltpu.SemaphoreType.DMA
    quarter = (HALF, HD)
    return pl.pallas_call(
        exchange_kernel,
        name="exchange",
        out_shape=(
            jax.ShapeDtypeStruct((SENT * BLK, QH * HD), bf16),
            jax.ShapeDtypeStruct((SENT * BLK, KV), bf16),
            jax.ShapeDtypeStruct((SHARD, KV), bf16),
        ),
        in_specs=[VMEM] * 4,
        out_specs=(VMEM, VMEM, VMEM),
        scratch_shapes=[
            pltpu.VMEM((NF, SHARD, KV), bf16),
            pltpu.VMEM((NF, SHARD, 2 * HD), bf16),
            pltpu.VMEM((NF, SHARD, 2 * HD), bf16),
            pltpu.VMEM((2 * CH, 2) + quarter, bf16),
            pltpu.VMEM((2 * CH, 2) + quarter, bf16),
            pltpu.VMEM((2 * CH, 2) + quarter, bf16),
            pltpu.VMEM((2 * CH, 2) + quarter, bf16),
            pltpu.VMEM((NF,) + quarter, bf16),
            pltpu.VMEM((2 * (NZ - 1),) + quarter, bf16),
            pltpu.VMEM((2,) + quarter, bf16),
            pltpu.VMEM((4,) + quarter, bf16),
            pltpu.VMEM(quarter, bf16),
            dma((64,)),
            dma((2,)),
            dma((CH,)),
            dma((2 * CH,)),
            dma((2 * CH,)),
            dma((2 * CH,)),
            dma((2 * (NZ - 1),)),
            dma((3,)),
            dma((7,)),
        ],
        compiler_params=pltpu.CompilerParams(
            collective_id=1, has_side_effects=True, vmem_limit_bytes=LIMIT
        ),
    )(inputs, kv_grad, query_pack, kv_pack)


STEPS = 7


def finish_kernel(
    flags_ref, kvg_ref, kvr_ref, w_ref, qg_ref, qr_ref, gw_ref, gi_out, gq_out, gw_out, chosen
):
    flags = [flags_ref[0, b] for b in range(NB)]
    ranks = handed_blocks(flags)[0]

    def select(own, other, b):
        at = jnp.minimum(ranks[b], SENT - 1) * BLK
        taken = other[pl.ds(pl.multiple_of(at, BLK), BLK), :]
        return jnp.where(flags[b] == 1, taken, own[b * BLK : (b + 1) * BLK, :])

    @pl.when(pl.program_id(0) == 0)
    def _():
        for b in range(NB):
            chosen[b * BLK : (b + 1) * BLK, :] = select(kvg_ref, kvr_ref, b)

    gi_out[...] = dot(chosen[...], w_ref[...], (1, 1)).astype(bf16)
    for b in range(NB):
        gq_out[b * BLK : (b + 1) * BLK, :] = select(qg_ref, qr_ref, b)
    gw_out[...] = gw_ref[...].astype(f32)


def finish(flags, kv_grad, kv_recv, weight, query_grad, query_recv, grad_weight):
    def across(rows, width):
        return pl.BlockSpec((rows, width), lambda n, *_: (0, n))

    def down(rows, width):
        return pl.BlockSpec((rows, width), lambda n, *_: (n, 0))

    wide, q_wide, deep = D // STEPS, QH * HD // STEPS, SHARD // STEPS
    return pl.pallas_call(
        finish_kernel,
        name="place_blocks",
        out_shape=(
            jax.ShapeDtypeStruct((ROWS, D), bf16),
            jax.ShapeDtypeStruct((ROWS, QH * HD), bf16),
            jax.ShapeDtypeStruct((SHARD, KV), f32),
        ),
        grid_spec=pltpu.PrefetchScalarGridSpec(
            num_scalar_prefetch=1,
            grid=(STEPS,),
            in_specs=[
                whole(ROWS, KV),
                whole(SENT * BLK, KV),
                down(wide, KV),
                across(ROWS, q_wide),
                across(SENT * BLK, q_wide),
                down(deep, KV),
            ],
            out_specs=(across(ROWS, wide), across(ROWS, q_wide), down(deep, KV)),
            scratch_shapes=[pltpu.VMEM((ROWS, KV), bf16)],
        ),
        compiler_params=pltpu.CompilerParams(vmem_limit_bytes=LIMIT),
    )(flags, kv_grad, kv_recv, weight, query_grad, query_recv, grad_weight)


def shards(inputs, queries, out_grad, kv_weight, passage_blocks, handover):
    weight = gather_weight(kv_weight)
    query_grad, query_pack, kv_grad, kv_pack = attend(
        inputs, queries, out_grad, weight, passage_blocks, handover
    )
    query_recv, kv_recv, share = exchange(inputs, kv_grad, query_pack, kv_pack)
    return finish(handover, kv_grad, kv_recv, weight, query_grad, query_recv, share)


def solution(mesh):
    rows = P(("dp", "fsdp"), None)
    return jax.shard_map(
        shards,
        mesh=mesh,
        in_specs=(rows, rows, rows, P("fsdp", None), rows, rows),
        out_specs=(rows, rows, P("fsdp", None)),
        check_vma=False,
    )
```

time: 522 us -> 113 us (0.22)
  waiting for transfers between devices: 423 us -> 0 us
  Pallas kernels: 0 us -> 109 us
  matrix products: 39.1 us -> 0 us
  local copies, waits for them, and re-layouts: 33.9 us -> 2.72 us
  between operations: 14 us -> 0.67 us
  other arithmetic: 9.06 us -> 0 us
    unnamed x4 -> x0, waiting for transfers between devices: 115 us -> none
    psum x1 -> x0, waiting for transfers between devices: 115 us -> none  [shards(): grad_weight = lax.psum(share, 'dp')]
    pallas_call x0 -> x4, Pallas kernels: none -> 109 us  [the longest x1 45.4 us: exchange(): pl.pallas_call(exchange_kernel, name='exchange', out_shape=(jax.ShapeDtyp...]
    ppermute x3 -> x0, waiting for transfers between devices: 102 us -> none  [from_partner(): return lax.ppermute(block, axis, route)]
    all_gather x1 -> x0, waiting for transfers between devices: 90.6 us -> none  [shards(): weight = lax.all_gather(kv_weight, 'fsdp', axis=0, tiled=True)]
    dot_general x10 -> x0, matrix products: 31.9 us -> none  [the longest x2 11.8 us: relocate(): jnp.einsum('bc,crw->brw', select.astype(own.dtype), other_blocks, preferr...]
    unnamed x31 -> x10, local copies, waits for them, and re-layouts: 20.5 us -> 2.72 us
    sub x1 -> x0, matrix products: 7.19 us -> none  [attend(): weights = jnp.exp(scores - top)]
  transfers between devices with their start and end apart: 6 -> 0, of which waited for: 4 -> 0; matrix products, arithmetic and copies ran while one was open for 8% -> 0% of each run, Pallas kernels for 0% -> 0%
where the time goes in v1:
time: 113 us; the launch traced here: 112 us
  Pallas kernels  109 us (96%)
  local copies, waits for them, and re-layouts  2.72 us (2%)
    pallas_call x1, Pallas kernels, exchange(): pl.pallas_call(exchange_kernel, name='exchange', out_shape=(jax.ShapeDtyp...  45.4 us
    pallas_call x1, Pallas kernels, gather_weight(): pl.pallas_call(gather_kernel, name='gather_weight', out_shape=jax.ShapeDt...  35.7 us
    pallas_call x1, Pallas kernels, attend(): pl.pallas_call(attend_kernel, name='attention_backward', out_shape=(jax.S...  20.1 us
    pallas_call x1, Pallas kernels, finish(): pl.pallas_call(finish_kernel, name='place_blocks', out_shape=(jax.ShapeDt...  7.82 us
    unnamed x10, local copies, waits for them, and re-layouts  2.72 us

profile of v1, /device:TPU:1, one launch (start us, length us, event | category | flops | bytes accessed | tf_op | source)
XLA Modules:
  0.0 112.4 jit_solution(3075891993575410824)
XLA Ops:
  0.6 0.0 copy-start.1
  0.6 0.9 copy-done.1
  1.6 0.0 copy-start.2
  1.6 0.0 copy-start.3
  1.6 0.0 copy-start.4
  1.6 35.7 %gather_weight.1 = bf16[2,8,224,512]{3,2,1,0:T(8,128)(2,1)S(1)} custom-call(bf16[224,512]{1,0:T(8,128)(2,1)S(1)} %copy-done.1), custom_call_target="tpu_custom_call" | custom-call | tf_op jit(solution)/shard_map/gather_weight/pallas_call | solution.py:138
  37.3 0.0 copy-start
  37.3 1.8 %copy-done = bf16[2,8,224,512]{3,2,1,0:T(8,128)(2,1)} copy-done((bf16[2,8,224,512]{3,2,1,0:T(8,128)(2,1)}, bf16[2,8,224,512]{3,2,1,0:T(8,128)(2,1)S(1)}, u32[]{:S(2)}) %copy-start) | copy-done | bytes 3670040
  39.1 0.0 copy-done.2
  39.1 0.0 copy-done.3
  39.1 0.0 copy-done.4
  39.1 20.1 %attention_backward.1 = (bf16[384,1792]{1,0:T(8,128)(2,1)S(1)}, bf16[320,1792]{1,0:T(8,128)(2,1)S(1)}, bf16[384,512]{1,0:T(8,128)(2,1)S(1)}, bf16[320,512]{1,0:T(8,128)(2,1)S(1)}) custom-call(s32[1,6]{1,0:T(1,128)S(1)} %copy-done.3, s32[1,6]{1,0:T(1,128)S(1)} %copy-done.2, bf16[384,3584]{1,0:T(8,128)(2,1)} %x_ref.3, bf16[3584,512]{1,0:T(8,128)(2,1)} %bitcast.1, ...), custom_call_target="tpu_custom_call" | custom-call | tf_op jit(solution)/shard_map/attention_backward/pallas_call | solution.py:255
  59.2 45.4 %exchange.1 = (bf16[320,1792]{1,0:T(8,128)(2,1)S(1)}, bf16[320,512]{1,0:T(8,128)(2,1)S(1)}, bf16[224,512]{1,0:T(8,128)(2,1)S(1)}) custom-call(bf16[384,3584]{1,0:T(8,128)(2,1)} %x_ref.3, bf16[384,512]{1,0:T(8,128)(2,1)S(1)} %get-tuple-element.10.kvg_ref, bf16[320,1792]{1,0:T(8,128)(2,1)S(1)} %get-tuple-element.11.qp_ref, ...), custom_call_target="tpu_custom_call" | custom-call | tf_op jit(solution)/shard_map/exchange/pallas_call | solution.py:451
  104.6 7.8 %place_blocks.1 = (bf16[384,3584]{1,0:T(8,128)(2,1)}, bf16[384,1792]{1,0:T(8,128)(2,1)}, f32[224,512]{1,0:T(8,128)}) custom-call(s32[1,6]{1,0:T(1,128)S(1)} %copy-done.2, bf16[384,512]{1,0:T(8,128)(2,1)S(1)} %get-tuple-element.10.kvg_ref, bf16[320,512]{1,0:T(8,128)(2,1)S(1)} %get-tuple-element.13.kvr_ref, bf16[3584,512]{1,0:T(8,128)(2,1)} %bitcast.2, ...), custom_call_target="tpu_custom_call" | custom-call | tf_op jit(solution)/shard_map/place_blocks/pallas_call | solution.py:523
Async XLA Ops:
  0.6 0.9 copy-start.1
  1.6 37.5 %copy-start.2 = (s32[1,6]{1,0:T(1,128)S(1)}, s32[1,6]{1,0:T(1,128)}, u32[]{:S(2)}) copy-start(s32[1,6]{1,0:T(1,128)} %flags_ref.3) | copy-start | bytes 76
  1.6 37.5 %copy-start.3 = (s32[1,6]{1,0:T(1,128)S(1)}, s32[1,6]{1,0:T(1,128)}, u32[]{:S(2)}) copy-start(s32[1,6]{1,0:T(1,128)} %ids_ref.1) | copy-start | bytes 76
  1.6 37.5 %copy-start.4 = (f32[1,128]{1,0:T(1,128)S(1)}, f32[1,128]{1,0:T(1,128)}, u32[]{:S(2)}) copy-start(f32[1,128]{1,0:T(1,128)} %constant.2.clone.freq_ref) | copy-start | bytes 1540
  37.3 1.8 %copy-start = (bf16[2,8,224,512]{3,2,1,0:T(8,128)(2,1)}, bf16[2,8,224,512]{3,2,1,0:T(8,128)(2,1)S(1)}, u32[]{:S(2)}) copy-start(bf16[2,8,224,512]{3,2,1,0:T(8,128)(2,1)S(1)} %gather_weight.1) | copy-start | bytes 11010052

commit v2 on v0

v2 whole, which is shorter than its diff:
```python
import jax
import jax.numpy as jnp
import numpy as np
from jax import lax
from jax.experimental import pallas as pl
from jax.experimental.pallas import tpu as pltpu
from jax.sharding import PartitionSpec as P

KVH = 2
GROUP = 7
HD = 128
QH = 14
NB = 6
BLK = 64
SENT = NB - 1
ROWS = NB * BLK
D = 3584
NX, NZ, NF = 4, 8, 16
SHARD = D // NF
HALF = SHARD // 2
CHUNK = 4 * SHARD
KV = 2 * KVH * HD
ROPE_BASE = 1000000.0
MESH = pl.DeviceIdType.MESH
VMEM = pl.BlockSpec(memory_space=pltpu.VMEM)
LIMIT = 56 * 1024 * 1024
f32, bf16 = jnp.float32, jnp.bfloat16


def place():
    d, f = lax.axis_index("dp"), lax.axis_index("fsdp")
    return d // 8, (d // 2) % NX, d % 2, f // NZ, f % NZ


def device(lo, x, c, hi, z):
    return (lo * 8 + x * 2 + c, hi * NZ + z)


def greet(peers):
    barrier = pltpu.get_barrier_semaphore()
    for peer in peers:
        pl.semaphore_signal(barrier, inc=1, device_id=peer, device_id_type=MESH)
    pl.semaphore_wait(barrier, len(peers))


def columns(index, width=HD):
    return pl.ds(pl.multiple_of(index * width, width), width)


def dot(a, b, dims):
    return lax.dot_general(a, b, ((dims[:1], dims[1:]), ((), ())), preferred_element_type=f32)


def handed_blocks(flags):
    rank, ranks = jnp.int32(0), []
    for b in range(NB):
        ranks.append(rank)
        rank = rank + flags[b]
    picks = []
    for r in range(SENT):
        pick = jnp.int32(0)
        for b in range(NB):
            pick = jnp.where((flags[b] == 1) & (ranks[b] == r), b, pick)
        picks.append(pick)
    return ranks, picks


HOPS = {1: 4, -1: 3}
WAYS = [(1, 1), (-1, 1), (1, 2), (-1, 2), (1, 3), (-1, 3), (1, 4)]


def kernel(
    ids_ref, flags_ref, w_ref, freq_ref, x_hbm, q_hbm, g_hbm,
    gi_hbm, gq_hbm, gw_hbm,
    x_ref, q_ref, g_ref, x_t, weight,
    keys, keys_t, vals, kacc, vacc, bias, cosine, sine, to_pack, from_pack, kept,
    qg, qp, qr, kvg, kvp, kvr, chosen, gi, gq, gw,
    part, sib, tot, relay_in, relay_out, direct, summed, after_x, z_in, after_z, y_in, final, shared,
    load, store, g_send, ring_recv, gy_recv, gx_recv, near_recv, far_recv,
    q_send, q_recv, kv_send, kv_recv,
    d_send, sib_recv, relay_recv, direct_recv, summed_recv, z_recv, y_recv, share_send, share_recv,
):
    lo, x, c, hi, z = place()
    y = 2 * hi + lo
    oth = 1 - hi
    sibling = device(lo, x, 1 - c, hi, z)
    partner = device(1 - lo, x, c, hi, z)
    cross = device(1 - lo, x, c, oth, z)
    across = device(lo, x, c, oth, z)
    x_side = ((x + 1) % NX, (x + NX - 1) % NX)
    x_peer = [device(lo, xs, c, hi, z) for xs in x_side]
    z_peer = [device(lo, x, c, hi, (z + s) % NZ) for s in range(1, NZ)]
    row_peer = [
        device(lo, (x + dx) % NX, (c + dc) % 2, hi, z)
        for dx in range(NX)
        for dc in range(2)
        if dx or dc
    ]
    loads = [
        pltpu.make_async_copy(src, dst, load.at[at])
        for at, (src, dst) in enumerate(((x_hbm, x_ref), (q_hbm, q_ref), (g_hbm, g_ref)))
    ]
    for copy in loads:
        copy.start()
    for q in range(2 * KVH):
        weight[q, hi, z] = w_ref[:, q * HD : (q + 1) * HD]
    greet(row_peer + z_peer + [partner, cross, across])

    def remote(src, dst, peer, sent, recv):
        return pltpu.make_async_remote_copy(
            src_ref=src,
            dst_ref=dst,
            send_sem=sent,
            recv_sem=recv,
            device_id=peer,
            device_id_type=MESH,
        )

    def pusher(sems):
        started = []

        def push(src, dst, peer, recv):
            copy = remote(src, dst, peer, sems.at[len(started)], recv)
            copy.start()
            started.append(copy)

        return push, started

    def arrived(dst, recv):
        remote(dst, dst, sibling, g_send.at[0], recv).wait_recv()

    ids = [ids_ref[0, b] for b in range(NB)]
    flags = [flags_ref[0, b] for b in range(NB)]
    ranks, picks = handed_blocks(flags)

    def set_masks():
        tall = lax.broadcasted_iota(jnp.int32, (ROWS, ROWS), 0)
        wide = lax.broadcasted_iota(jnp.int32, (ROWS, ROWS), 1)
        label_k = jnp.zeros((ROWS, ROWS), jnp.int32)
        label_q = jnp.zeros((ROWS, ROWS), jnp.int32)
        for b in range(NB):
            label_k = jnp.where(tall >= b * BLK, ids[b], label_k)
            label_q = jnp.where(wide >= b * BLK, ids[b], label_q)
        bias[...] = jnp.where(label_k == label_q, 0.0, -jnp.inf)

    def set_moves():
        tall = lax.broadcasted_iota(jnp.int32, (SENT * BLK, ROWS), 0)
        wide = lax.broadcasted_iota(jnp.int32, (SENT * BLK, ROWS), 1)
        shift = jnp.zeros((SENT * BLK, ROWS), jnp.int32)
        for r in range(SENT):
            shift = jnp.where(tall >= r * BLK, (picks[r] - r) * BLK, shift)
        to_pack[...] = jnp.where(tall + shift == wide, 1.0, 0.0).astype(bf16)
        tall = lax.broadcasted_iota(jnp.int32, (ROWS, SENT * BLK), 0)
        wide = lax.broadcasted_iota(jnp.int32, (ROWS, SENT * BLK), 1)
        shift = jnp.zeros((ROWS, SENT * BLK), jnp.int32)
        for b in range(NB):
            shift = jnp.where(tall >= b * BLK, (ranks[b] - b) * BLK, shift)
        from_pack[...] = jnp.where(tall + shift == wide, 1.0, 0.0).astype(bf16)
        row = lax.broadcasted_iota(jnp.int32, (ROWS, HD), 0)
        given = jnp.zeros((ROWS, HD), jnp.int32)
        for b in range(NB):
            given = jnp.where(row >= b * BLK, flags[b], given)
        kept[...] = (1 - given).astype(f32)

    def set_angles():
        first = [jnp.int32(0)]
        for b in range(1, NB):
            first.append(jnp.where(ids[b] == ids[b - 1], first[b - 1], b * BLK))
        row = lax.broadcasted_iota(jnp.int32, (ROWS, HD), 0)
        start = jnp.zeros((ROWS, HD), jnp.int32)
        for b in range(NB):
            start = jnp.where(row >= b * BLK, first[b], start)
        angle = (row - start).astype(f32) * freq_ref[...]
        cosine[...] = jnp.cos(angle)
        lane = lax.broadcasted_iota(jnp.int32, (ROWS, HD), 1)
        turn = jnp.sin(angle)
        sine[...] = jnp.where(lane < HD // 2, -turn, turn)

    def turn_inputs(first, count):
        @pl.loop(first, first + count)
        def _(n):
            x_t[pl.ds(pl.multiple_of(n * HD, HD), HD), :] = x_ref[:, columns(n)].T

    def piece_1():
        loads[0].wait()
        turn_inputs(0, 7)

    def piece_2():
        set_masks()
        turn_inputs(7, 7)

    def piece_3():
        set_angles()
        set_moves()

    def piece_4():
        turn_inputs(14, 14)

    pieces = {1: piece_1, 2: piece_2, 3: piece_3, 4: piece_4}

    near = 2 * (x % 2) + c
    far = 2 * (1 - x % 2) + c
    push, gather_started = pusher(g_send)

    def source(way, hop):
        return (z + NZ - way * hop) % NZ

    def slot(way, hop):
        return 7 if hop == 0 else WAYS.index((way, hop))

    def from_ring(way, hop):
        part = weight.at[near, hi, source(way, hop)]
        at = slot(way, hop)
        arrived(part, ring_recv.at[at])
        if hop < HOPS[way]:
            push(part, part, z_peer[0 if way == 1 else 6], ring_recv.at[slot(way, hop + 1)])
        push(part, part, cross, gy_recv.at[at])
        push(part, part, x_peer[0 if way == 1 else 1], gx_recv.at[at])
        push(part, part, sibling, near_recv.at[at])

    def from_y(way, hop):
        part = weight.at[near, oth, source(way, hop)]
        at = slot(way, hop)
        arrived(part, gy_recv.at[at])
        push(part, part, x_peer[1 if way == 1 and hop else 0], gx_recv.at[8 + at])
        push(part, part, sibling, near_recv.at[8 + at])

    def from_x(row, half, way, hop):
        part = weight.at[far, row, source(way, hop)]
        at = half * 8 + slot(way, hop)
        arrived(part, gx_recv.at[at])
        push(part, part, sibling, far_recv.at[at])

    own = weight.at[near, hi, z]
    push(own, own, z_peer[0], ring_recv.at[slot(1, 1)])
    push(own, own, z_peer[6], ring_recv.at[slot(-1, 1)])
    push(own, own, cross, gy_recv.at[slot(1, 0)])
    for time in range(1, 7):
        for way in (1, -1):
            if time <= HOPS[way]:
                from_ring(way, time)
        if time == 1:
            from_y(1, 0)
        for way in (1, -1):
            if 1 <= time - 1 <= HOPS[way]:
                from_y(way, time - 1)
        if time == 2:
            from_x(oth, 1, 1, 0)
        for way in (1, -1):
            if 1 <= time - 1 <= HOPS[way]:
                from_x(hi, 0, way, time - 1)
            if 1 <= time - 2 <= HOPS[way]:
                from_x(oth, 1, way, time - 2)
        if time in pieces:
            pieces[time]()
    for half, row in ((0, hi), (1, oth)):
        for way, hop in WAYS + [(1, 0)] * half:
            at = half * 8 + slot(way, hop)
            arrived(weight.at[2 * (x % 2) + 1 - c, row, source(way, hop)], near_recv.at[at])
            arrived(weight.at[2 * (1 - x % 2) + 1 - c, row, source(way, hop)], far_recv.at[at])

    def weight_rows(n):
        at = pl.ds((n % 2) * 4, 4)
        return jnp.concatenate(
            [weight[q, n // 2, at].reshape(CHUNK, HD) for q in range(2 * KVH)], axis=1
        )

    projected = jnp.zeros((ROWS, KV), f32)
    for n in range(4):
        projected += dot(x_ref[:, n * CHUNK : (n + 1) * CHUNK], weight_rows(n), (1, 0))
    for g in range(KVH):
        raw = projected[:, g * HD : (g + 1) * HD]
        key = raw * cosine[...] + pltpu.roll(raw, HD // 2, 1) * sine[...]
        keys[g] = key.astype(bf16)
        keys_t[g] = key.T.astype(bf16)
        vals[g] = projected[:, (KVH + g) * HD : (KVH + g + 1) * HD].astype(bf16)
    loads[1].wait()
    loads[2].wait()

    scale = 1.0 / HD**0.5

    def hand_over(h):
        return remote(qp.at[h], qr.at[h], partner, q_send.at[h], q_recv.at[h])

    def heads(g, first, last, send_now):
        @pl.loop(first, last)
        def _(h):
            query, grad = q_ref[:, columns(h)], g_ref[:, columns(h)]
            scores = dot(keys[g], query, (1, 1)) * scale + bias[...]
            weights = jnp.exp(scores - jnp.max(scores, axis=0, keepdims=True))
            probs = weights * (1.0 / jnp.sum(weights, axis=0, keepdims=True))
            probs_b = probs.astype(bf16)
            dprobs = dot(vals[g], grad, (1, 1))
            delta = jnp.sum(probs_b.astype(f32) * dprobs, axis=0, keepdims=True)
            dscores_b = (probs * (dprobs - delta)).astype(bf16)
            vacc[...] += dot(probs_b, grad, (1, 0))
            kacc[...] += dot(dscores_b, query, (1, 0))
            query_grad = dot(keys_t[g], dscores_b, (1, 0)) * scale
            own = query_grad.T.astype(bf16)
            qg[h] = own
            qp[h] = dot(to_pack[...], own, (1, 0)).astype(bf16)
            if send_now:
                hand_over(h).start()

    def clear():
        kacc[...] = jnp.zeros_like(kacc)
        vacc[...] = jnp.zeros_like(vacc)

    def hand_over_kv(g):
        return remote(kvp.at[g], kvr.at[g], partner, kv_send.at[g], kv_recv.at[g])

    def finish_group(g):
        grad_k = kacc[...] * scale
        raw = grad_k * cosine[...] - pltpu.roll(grad_k, HD // 2, 1) * sine[...]
        kvg[g, 0] = raw.astype(bf16)
        kvg[g, 1] = vacc[...].astype(bf16)
        for t in range(2):
            kvp[g, t] = dot(to_pack[...], kvg[g, t], (1, 0)).astype(bf16)
        hand_over_kv(g).start()

    push_d, d_started = pusher(d_send)

    def product(g):
        pair = jnp.concatenate([kvg[g, 0], kvg[g, 1]], axis=1)
        for n in range(4):
            result = dot(x_t[n * CHUNK : (n + 1) * CHUNK, :], pair, (1, 0)).astype(bf16)
            for t in range(2):
                half = result[:, t * HD : (t + 1) * HD]
                part[g, t, n * 4 : (n + 1) * 4] = half.reshape(4, SHARD, HD)
            four = pl.ds(n * 4, 4)
            push_d(part.at[g, 1 - c, four], sib.at[g, four], sibling, sib_recv.at[g * 4 + n])

    def box(xs, side):
        owners = pl.ds((xs % 2) * NZ + 4 * side, 4)
        return owners, pl.ds(pl.multiple_of((xs // 2) * HALF, HALF), HALF)

    def core_sum(g):
        for n in range(4):
            four = pl.ds(n * 4, 4)
            arrived(sib.at[g, four], sib_recv.at[g * 4 + n])
            total = part[g, c, four].astype(f32) + sib[g, four].astype(f32)
            tot[g, four] = total.astype(bf16)
        for side in range(2):
            at = 2 * g + side
            owners, rows = box((x + 2) % NX, side)
            push_d(tot.at[g, owners, rows], relay_in.at[at], x_peer[side], relay_recv.at[at])
        for side in range(2):
            at = 2 * g + side
            owners, rows = box(x_side[side], 1 - side)
            push_d(tot.at[g, owners, rows], direct.at[at], x_peer[side], direct_recv.at[at])

    def relay(g):
        for side in range(2):
            at = 2 * g + side
            owners, rows = box(x_side[side], side)
            arrived(relay_in.at[at], relay_recv.at[at])
            total = tot[g, owners, rows].astype(f32) + relay_in[at].astype(f32)
            relay_out[at] = total.astype(bf16)
            push_d(relay_out.at[at], summed.at[at], x_peer[side], summed_recv.at[at])

    def x_sum(g):
        for side in range(2):
            at, other = 2 * g + side, 2 * g + 1 - side
            owners, rows = box(x, side)
            arrived(direct.at[other], direct_recv.at[other])
            arrived(summed.at[at], summed_recv.at[at])
            got = summed[at].astype(f32) + direct[other].astype(f32)
            total = tot[g, owners, rows].astype(f32) + got
            after_x[g, side * 4 : (side + 1) * 4] = total.astype(bf16)
        for s in range(1, NZ):
            at = g * (NZ - 1) + s - 1
            push_d(after_x.at[g, (z + s) % NZ], z_in.at[at], z_peer[s - 1], z_recv.at[at])

    def z_sum(g):
        total = after_x[g, z].astype(f32)
        for s in range(1, NZ):
            at = g * (NZ - 1) + s - 1
            arrived(z_in.at[at], z_recv.at[at])
            total = total + z_in[at].astype(f32)
        after_z[g] = total.astype(bf16)
        y_in[g, y] = after_z[g]
        for n, peer in enumerate((partner, cross, across)):
            push_d(after_z.at[g], y_in.at[g, y], peer, y_recv.at[3 * g + n])

    def share(g):
        return [
            remote(
                final.at[g],
                shared.at[g, x // 2, c],
                peer,
                share_send.at[g * 7 + n],
                share_recv.at[g * 4 + (x // 2) * 2 + c],
            )
            for n, peer in enumerate(row_peer)
        ]

    def y_sum(g):
        arrived(y_in.at[g, 2 * hi + 1 - lo], y_recv.at[3 * g])
        arrived(y_in.at[g, 2 * oth + 1 - lo], y_recv.at[3 * g + 1])
        arrived(y_in.at[g, 2 * oth + lo], y_recv.at[3 * g + 2])
        total = y_in[g, 0].astype(f32)
        for at in range(1, 4):
            total = total + y_in[g, at].astype(f32)
        final[g] = total.astype(bf16)

        @pl.when(x % 2 == hi)
        def _():
            shared[g, x // 2, c] = final[g]
            for copy in share(g):
                copy.start()

    def collect(g):
        for half in range(2):
            for core in range(2):
                mine = (x % 2 == hi) & (x // 2 == half) & (c == core)

                @pl.when(jnp.logical_not(mine))
                def _():
                    at = g * 4 + half * 2 + core
                    arrived(shared.at[g, half, core], share_recv.at[at])

                gw[half * HALF : (half + 1) * HALF, (core * KVH + g) * HD : (core * KVH + g + 1) * HD] = (
                    shared[g, half, core].astype(f32)
                )

    stores = []

    def put(src, dst):
        copy = pltpu.make_async_copy(src, dst, store.at[len(stores)])
        copy.start()
        stores.append(copy)

    def pick(own, other):
        taken = dot(from_pack[...], other, (1, 0))
        return jnp.where(kept[...] > 0.5, own.astype(f32), taken).astype(bf16)

    def input_grad():
        for g in range(KVH):
            arrived(kvr.at[g], kv_recv.at[g])
        for g in range(KVH):
            for t in range(2):
                at = (t * KVH + g) * HD
                chosen[:, at : at + HD] = pick(kvg[g, t], kvr[g, t])
        for n in range(4):
            cols = slice(n * CHUNK, (n + 1) * CHUNK)
            gi[:, cols] = dot(chosen[...], weight_rows(n), (1, 1)).astype(bf16)
            put(gi.at[:, cols], gi_hbm.at[:, cols])

    def place_queries(first, last):
        @pl.loop(first, last)
        def _(h):
            arrived(qr.at[h], q_recv.at[h])
            gq[:, columns(h)] = pick(qg[h], qr[h])

        cols = slice(first * HD, last * HD)
        put(gq.at[:, cols], gq_hbm.at[:, cols])

    clear()
    heads(0, 0, 7, True)
    finish_group(0)
    clear()
    product(0)
    heads(1, 7, 9, True)
    core_sum(0)
    heads(1, 9, 11, False)
    relay(0)
    heads(1, 11, 13, False)
    x_sum(0)
    heads(1, 13, 14, False)
    finish_group(1)
    for h in range(9, 14):
        hand_over(h).start()
    product(1)
    core_sum(1)
    z_sum(0)
    relay(1)
    y_sum(0)
    x_sum(1)
    input_grad()
    z_sum(1)
    place_queries(0, 7)
    collect(0)
    y_sum(1)
    place_queries(7, 14)
    collect(1)
    put(gw, gw_hbm)
    for copy in gather_started + d_started:
        copy.wait_send()
    for h in range(QH):
        hand_over(h).wait_send()
    for g in range(KVH):
        hand_over_kv(g).wait_send()

        @pl.when(x % 2 == hi)
        def _():
            for copy in share(g):
                copy.wait_send()

    for copy in stores:
        copy.wait()


def shards(inputs, queries, out_grad, kv_weight, passage_blocks, handover):
    freq = ROPE_BASE ** (-(np.arange(HD // 2, dtype=np.float32) * 2.0) / HD)
    freq = jnp.asarray(np.concatenate([freq, freq])[None, :].astype(np.float32))
    dma = pltpu.SemaphoreType.DMA
    anywhere = pl.BlockSpec(memory_space=pl.ANY)
    scalars = pl.BlockSpec(memory_space=pltpu.SMEM)

    def vmem(*shape, kind=bf16):
        return pltpu.VMEM(shape, kind)

    packed = SENT * BLK
    return pl.pallas_call(
        kernel,
        name="grouped_attention_backward",
        out_shape=(
            jax.ShapeDtypeStruct((ROWS, D), bf16),
            jax.ShapeDtypeStruct((ROWS, QH * HD), bf16),
            jax.ShapeDtypeStruct((SHARD, KV), f32),
        ),
        in_specs=[scalars, scalars, VMEM, VMEM, anywhere, anywhere, anywhere],
        out_specs=(anywhere, anywhere, anywhere),
        scratch_shapes=[
            vmem(ROWS, D),
            vmem(ROWS, QH * HD),
            vmem(ROWS, QH * HD),
            vmem(D, ROWS),
            vmem(2 * KVH, 2, NZ, SHARD, HD),
            vmem(KVH, ROWS, HD),
            vmem(KVH, HD, ROWS),
            vmem(KVH, ROWS, HD),
            vmem(ROWS, HD, kind=f32),
            vmem(ROWS, HD, kind=f32),
            vmem(ROWS, ROWS, kind=f32),
            vmem(ROWS, HD, kind=f32),
            vmem(ROWS, HD, kind=f32),
            vmem(packed, ROWS),
            vmem(ROWS, packed),
            vmem(ROWS, HD, kind=f32),
            vmem(QH, ROWS, HD),
            vmem(QH, packed, HD),
            vmem(QH, packed, HD),
            vmem(KVH, 2, ROWS, HD),
            vmem(KVH, 2, packed, HD),
            vmem(KVH, 2, packed, HD),
            vmem(ROWS, KV),
            vmem(ROWS, D),
            vmem(ROWS, QH * HD),
            vmem(SHARD, KV, kind=f32),
            vmem(KVH, 2, NF, SHARD, HD),
            vmem(KVH, NF, SHARD, HD),
            vmem(KVH, NF, SHARD, HD),
            vmem(2 * KVH, 4, HALF, HD),
            vmem(2 * KVH, 4, HALF, HD),
            vmem(2 * KVH, 4, HALF, HD),
            vmem(2 * KVH, 4, HALF, HD),
            vmem(KVH, NZ, HALF, HD),
            vmem(KVH * (NZ - 1), HALF, HD),
            vmem(KVH, HALF, HD),
            vmem(KVH, 4, HALF, HD),
            vmem(KVH, HALF, HD),
            vmem(KVH, 2, 2, HALF, HD),
            dma((3,)),
            dma((8,)),
            dma((64,)),
            dma((8,)),
            dma((8,)),
            dma((16,)),
            dma((16,)),
            dma((16,)),
            dma((QH,)),
            dma((QH,)),
            dma((KVH,)),
            dma((KVH,)),
            dma((48,)),
            dma((8,)),
            dma((4,)),
            dma((4,)),
            dma((4,)),
            dma((KVH * (NZ - 1),)),
            dma((6,)),
            dma((14,)),
            dma((8,)),
        ],
        compiler_params=pltpu.CompilerParams(
            collective_id=0, has_side_effects=True, vmem_limit_bytes=LIMIT
        ),
    )(passage_blocks, handover, kv_weight, freq, inputs, queries, out_grad)

def solution(mesh):
    rows = P(("dp", "fsdp"), None)
    return jax.shard_map(
        shards,
        mesh=mesh,
        in_specs=(rows, rows, rows, P("fsdp", None), rows, rows),
        out_specs=(rows, rows, P("fsdp", None)),
        check_vma=False,
    )
```

time: 522 us -> 102 us (0.20)
  waiting for transfers between devices: 423 us -> 0 us
  Pallas kernels: 0 us -> 95.5 us
  matrix products: 39.1 us -> 0 us
  local copies, waits for them, and re-layouts: 33.9 us -> 5.69 us
  between operations: 14 us -> 0.65 us
  other arithmetic: 9.06 us -> 0 us
    unnamed x4 -> x0, waiting for transfers between devices: 115 us -> none
    psum x1 -> x0, waiting for transfers between devices: 115 us -> none  [shards(): grad_weight = lax.psum(share, 'dp')]
    ppermute x3 -> x0, waiting for transfers between devices: 102 us -> none  [from_partner(): return lax.ppermute(block, axis, route)]
    pallas_call x0 -> x1, Pallas kernels: none -> 95.5 us  [shards(): pl.pallas_call(kernel, name='grouped_attention_backward', out_shape=(jax....]
    all_gather x1 -> x0, waiting for transfers between devices: 90.6 us -> none  [shards(): weight = lax.all_gather(kv_weight, 'fsdp', axis=0, tiled=True)]
    dot_general x10 -> x0, matrix products: 31.9 us -> none  [the longest x2 11.8 us: relocate(): jnp.einsum('bc,crw->brw', select.astype(own.dtype), other_blocks, preferr...]
    unnamed x31 -> x7, local copies, waits for them, and re-layouts: 20.5 us -> 5.69 us
    sub x1 -> x0, matrix products: 7.19 us -> none  [attend(): weights = jnp.exp(scores - top)]
  transfers between devices with their start and end apart: 6 -> 0, of which waited for: 4 -> 0; matrix products, arithmetic and copies ran while one was open for 8% -> 0% of each run, Pallas kernels for 0% -> 0%
where the time goes in v2:
time: 102 us
  Pallas kernels  95.5 us (94%)
  local copies, waits for them, and re-layouts  5.69 us (6%)
    pallas_call x1, Pallas kernels, shards(): pl.pallas_call(kernel, name='grouped_attention_backward', out_shape=(jax....  95.5 us
    unnamed x7, local copies, waits for them, and re-layouts  5.69 us

profile of v2, /device:TPU:1, one launch (start us, length us, event | category | flops | bytes accessed | tf_op | source)
XLA Modules:
  0.0 101.8 jit_solution(5006662061998229951)
XLA Ops:
  0.6 95.5 %grouped_attention_backward.1 = (bf16[384,3584]{1,0:T(8,128)(2,1)}, bf16[384,1792]{1,0:T(8,128)(2,1)}, f32[224,512]{1,0:T(8,128)}) custom-call(s32[1,6]{1,0:T(1,128)} %ids_ref.1, s32[1,6]{1,0:T(1,128)} %flags_ref.1, bf16[224,512]{1,0:T(8,128)(2,1)} %w_ref.1, f32[1,128]{1,0:T(1,128)} %constant.2.clone.freq_ref, bf16[384,3584]{1,0:T(8,128)(2,1)} %x_hbm.1, ...), custom_call_target="tpu_custom_call" | custom-call | tf_op jit(solution)/shard_map/grouped_attention_backward/pallas_call | solution.py:514
  96.1 0.0 copy-start
  96.1 3.6 %copy.13 = bf16[384,3584]{1,0:T(8,128)(2,1)} copy(bf16[384,3584]{1,0:T(8,128)(2,1)} %get-tuple-element.6) | data formatting | bytes 5505024
  99.7 0.0 copy-done
  99.7 0.0 copy-start.1
  99.7 1.1 %copy.14 = bf16[384,1792]{1,0:T(8,128)(2,1)} copy(bf16[384,1792]{1,0:T(8,128)(2,1)S(1)} %copy-done) | data formatting | bytes 2752512
  100.8 0.2 copy-done.1
  101.0 0.8 copy.15
Async XLA Ops:
  96.1 3.6 %copy-start = (bf16[384,1792]{1,0:T(8,128)(2,1)S(1)}, bf16[384,1792]{1,0:T(8,128)(2,1)}, u32[]{:S(2)}) copy-start(bf16[384,1792]{1,0:T(8,128)(2,1)} %get-tuple-element.7) | copy-start | bytes 4128772
  99.7 1.3 %copy-start.1 = (f32[224,512]{1,0:T(8,128)S(1)}, f32[224,512]{1,0:T(8,128)}, u32[]{:S(2)}) copy-start(f32[224,512]{1,0:T(8,128)} %get-tuple-element.8) | copy-start | bytes 1376260

commit v3 on v2

--- a/solution.py
+++ b/solution.py
@@ -66,6 +66,7 @@
 
 
 HOPS = {1: 4, -1: 3}
+ARRIVES = {1: 2, 2: 1, 3: 3, 4: 4}
 WAYS = [(1, 1), (-1, 1), (1, 2), (-1, 2), (1, 3), (-1, 3), (1, 4)]
 
 
@@ -181,20 +182,22 @@
         def _(n):
             x_t[pl.ds(pl.multiple_of(n * HD, HD), HD), :] = x_ref[:, columns(n)].T
 
+    def piece_0():
+        set_masks()
+        set_moves()
+
     def piece_1():
         loads[0].wait()
-        turn_inputs(0, 7)
+        turn_inputs(0, 6)
 
     def piece_2():
-        set_masks()
-        turn_inputs(7, 7)
+        turn_inputs(6, 6)
 
     def piece_3():
         set_angles()
-        set_moves()
 
     def piece_4():
-        turn_inputs(14, 14)
+        turn_inputs(12, 16)
 
     pieces = {1: piece_1, 2: piece_2, 3: piece_3, 4: piece_4}
 
@@ -212,8 +215,10 @@
         part = weight.at[near, hi, source(way, hop)]
         at = slot(way, hop)
         arrived(part, ring_recv.at[at])
-        if hop < HOPS[way]:
-            push(part, part, z_peer[0 if way == 1 else 6], ring_recv.at[slot(way, hop + 1)])
+        if hop == 2:
+            push(part, part, z_peer[0 if way == 1 else 6], ring_recv.at[slot(way, 3)])
+            if way == 1:
+                push(part, part, z_peer[1], ring_recv.at[slot(way, 4)])
         push(part, part, cross, gy_recv.at[at])
         push(part, part, x_peer[0 if way == 1 else 1], gx_recv.at[at])
         push(part, part, sibling, near_recv.at[at])
@@ -232,25 +237,28 @@
         push(part, part, sibling, far_recv.at[at])
 
     own = weight.at[near, hi, z]
+    push(own, own, z_peer[1], ring_recv.at[slot(1, 2)])
+    push(own, own, z_peer[5], ring_recv.at[slot(-1, 2)])
     push(own, own, z_peer[0], ring_recv.at[slot(1, 1)])
     push(own, own, z_peer[6], ring_recv.at[slot(-1, 1)])
     push(own, own, cross, gy_recv.at[slot(1, 0)])
+    piece_0()
     for time in range(1, 7):
         for way in (1, -1):
-            if time <= HOPS[way]:
-                from_ring(way, time)
-        if time == 1:
+            if time in ARRIVES and ARRIVES[time] <= HOPS[way]:
+                from_ring(way, ARRIVES[time])
+        if time == 2:
             from_y(1, 0)
         for way in (1, -1):
-            if 1 <= time - 1 <= HOPS[way]:
-                from_y(way, time - 1)
-        if time == 2:
+            if time - 1 in ARRIVES and ARRIVES[time - 1] <= HOPS[way]:
+                from_y(way, ARRIVES[time - 1])
+        if time == 3:
             from_x(oth, 1, 1, 0)
         for way in (1, -1):
-            if 1 <= time - 1 <= HOPS[way]:
-                from_x(hi, 0, way, time - 1)
-            if 1 <= time - 2 <= HOPS[way]:
-                from_x(oth, 1, way, time - 2)
+            if time - 1 in ARRIVES and ARRIVES[time - 1] <= HOPS[way]:
+                from_x(hi, 0, way, ARRIVES[time - 1])
+            if time - 2 in ARRIVES and ARRIVES[time - 2] <= HOPS[way]:
+                from_x(oth, 1, way, ARRIVES[time - 2])
         if time in pieces:
             pieces[time]()
     for half, row in ((0, hi), (1, oth)):
@@ -283,9 +291,8 @@
         return remote(qp.at[h], qr.at[h], partner, q_send.at[h], q_recv.at[h])
 
     def heads(g, first, last, send_now):
-        @pl.loop(first, last)
-        def _(h):
-            query, grad = q_ref[:, columns(h)], g_ref[:, columns(h)]
+        for h in range(first, last):
+            query, grad = q_ref[:, h * HD : (h + 1) * HD], g_ref[:, h * HD : (h + 1) * HD]
             scores = dot(keys[g], query, (1, 1)) * scale + bias[...]
             weights = jnp.exp(scores - jnp.max(scores, axis=0, keepdims=True))
             probs = weights * (1.0 / jnp.sum(weights, axis=0, keepdims=True))
@@ -320,32 +327,34 @@
 
     push_d, d_started = pusher(d_send)
 
-    def product(g):
+    def chunk(i):
+        return 2 * (x % 2 if i < 2 else 1 - x % 2) + i % 2
+
+    def product(g, i):
+        n = chunk(i)
         pair = jnp.concatenate([kvg[g, 0], kvg[g, 1]], axis=1)
-        for n in range(4):
-            result = dot(x_t[n * CHUNK : (n + 1) * CHUNK, :], pair, (1, 0)).astype(bf16)
-            for t in range(2):
-                half = result[:, t * HD : (t + 1) * HD]
-                part[g, t, n * 4 : (n + 1) * 4] = half.reshape(4, SHARD, HD)
-            four = pl.ds(n * 4, 4)
-            push_d(part.at[g, 1 - c, four], sib.at[g, four], sibling, sib_recv.at[g * 4 + n])
+        rows = pl.ds(pl.multiple_of(n * CHUNK, CHUNK), CHUNK)
+        result = dot(x_t[rows, :], pair, (1, 0)).astype(bf16)
+        four = pl.ds(n * 4, 4)
+        for t in range(2):
+            part[g, t, four] = result[:, t * HD : (t + 1) * HD].reshape(4, SHARD, HD)
+        push_d(part.at[g, 1 - c, four], sib.at[g, four], sibling, sib_recv.at[g * 4 + i])
 
     def box(xs, side):
         owners = pl.ds((xs % 2) * NZ + 4 * side, 4)
         return owners, pl.ds(pl.multiple_of((xs // 2) * HALF, HALF), HALF)
 
-    def core_sum(g):
-        for n in range(4):
-            four = pl.ds(n * 4, 4)
-            arrived(sib.at[g, four], sib_recv.at[g * 4 + n])
-            total = part[g, c, four].astype(f32) + sib[g, four].astype(f32)
-            tot[g, four] = total.astype(bf16)
-        for side in range(2):
-            at = 2 * g + side
+    def core_sum(g, i):
+        four = pl.ds(chunk(i) * 4, 4)
+        arrived(sib.at[g, four], sib_recv.at[g * 4 + i])
+        total = part[g, c, four].astype(f32) + sib[g, four].astype(f32)
+        tot[g, four] = total.astype(bf16)
+        if i < 2:
+            side, at = i, 2 * g + i
             owners, rows = box((x + 2) % NX, side)
             push_d(tot.at[g, owners, rows], relay_in.at[at], x_peer[side], relay_recv.at[at])
-        for side in range(2):
-            at = 2 * g + side
+        else:
+            side, at = 3 - i, 2 * g + 3 - i
             owners, rows = box(x_side[side], 1 - side)
             push_d(tot.at[g, owners, rows], direct.at[at], x_peer[side], direct_recv.at[at])
 
@@ -459,28 +468,36 @@
     heads(0, 0, 7, True)
     finish_group(0)
     clear()
-    product(0)
-    heads(1, 7, 9, True)
-    core_sum(0)
-    heads(1, 9, 11, False)
+    for i in range(4):
+        product(0, i)
+    heads(1, 7, 8, True)
+    for i in range(4):
+        core_sum(0, i)
+    heads(1, 8, 9, True)
+    heads(1, 9, 12, False)
     relay(0)
-    heads(1, 11, 13, False)
-    x_sum(0)
-    heads(1, 13, 14, False)
+    heads(1, 12, 14, False)
     finish_group(1)
+    product(1, 0)
+    product(1, 1)
+    core_sum(1, 0)
+    product(1, 2)
+    core_sum(1, 1)
+    product(1, 3)
+    core_sum(1, 2)
+    core_sum(1, 3)
     for h in range(9, 14):
         hand_over(h).start()
-    product(1)
-    core_sum(1)
+    x_sum(0)
+    relay(1)
     z_sum(0)
-    relay(1)
-    y_sum(0)
     x_sum(1)
     input_grad()
+    y_sum(0)
     z_sum(1)
     place_queries(0, 7)
+    y_sum(1)
     collect(0)
-    y_sum(1)
     place_queries(7, 14)
     collect(1)
     put(gw, gw_hbm)
@@ -500,6 +517,19 @@
         copy.wait()
 
 
+def write_kernel(*refs):
+    sems, copies = refs[6], []
+    for src, dst, parts in zip(refs[:3], refs[3:6], (6, 3, 2)):
+        rows = src.shape[0] // parts
+        for n in range(parts):
+            at = pl.ds(n * rows, rows)
+            copies.append(pltpu.make_async_copy(src.at[at], dst.at[at], sems.at[len(copies)]))
+    for copy in copies:
+        copy.start()
+    for copy in copies:
+        copy.wait()
+
+
 def shards(inputs, queries, out_grad, kv_weight, passage_blocks, handover):
     freq = ROPE_BASE ** (-(np.arange(HD // 2, dtype=np.float32) * 2.0) / HD)
     freq = jnp.asarray(np.concatenate([freq, freq])[None, :].astype(np.float32))
@@ -511,14 +541,15 @@
         return pltpu.VMEM(shape, kind)
 
     packed = SENT * BLK
-    return pl.pallas_call(
+    shapes = (
+        jax.ShapeDtypeStruct((ROWS, D), bf16),
+        jax.ShapeDtypeStruct((ROWS, QH * HD), bf16),
+        jax.ShapeDtypeStruct((SHARD, KV), f32),
+    )
+    results = pl.pallas_call(
         kernel,
         name="grouped_attention_backward",
-        out_shape=(
-            jax.ShapeDtypeStruct((ROWS, D), bf16),
-            jax.ShapeDtypeStruct((ROWS, QH * HD), bf16),
-            jax.ShapeDtypeStruct((SHARD, KV), f32),
-        ),
+        out_shape=shapes,
         in_specs=[scalars, scalars, VMEM, VMEM, anywhere, anywhere, anywhere],
         out_specs=(anywhere, anywhere, anywhere),
         scratch_shapes=[
@@ -587,6 +618,14 @@
             collective_id=0, has_side_effects=True, vmem_limit_bytes=LIMIT
         ),
     )(passage_blocks, handover, kv_weight, freq, inputs, queries, out_grad)
+    return pl.pallas_call(
+        write_kernel,
+        name="write_results",
+        out_shape=shapes,
+        in_specs=[anywhere] * 3,
+        out_specs=(anywhere,) * 3,
+        scratch_shapes=[dma((16,))],
+    )(*results)
 
 def solution(mesh):
     rows = P(("dp", "fsdp"), None)

time: 102 us -> 228 us (2.24)
  Pallas kernels: 95.5 us -> 227 us
  local copies, waits for them, and re-layouts: 5.69 us -> 0 us
    pallas_call x1 -> x2, Pallas kernels: 95.5 us -> 227 us  [the longest x1 140 us: shards(): pl.pallas_call(write_kernel, name='write_results', out_shape=shapes, in_s...]
    unnamed x7 -> x0, local copies, waits for them, and re-layouts: 5.69 us -> none
where the time goes in v3:
time: 228 us
  Pallas kernels  227 us (100%)
    pallas_call x1, Pallas kernels, shards(): pl.pallas_call(write_kernel, name='write_results', out_shape=shapes, in_s...  140 us
    pallas_call x1, Pallas kernels, shards(): pl.pallas_call(kernel, name='grouped_attention_backward', out_shape=shape...  86.6 us

profile of v3, /device:TPU:1, one launch (start us, length us, event | category | flops | bytes accessed | tf_op | source)
XLA Modules:
  0.0 227.6 jit_solution(13591032053288566898)
XLA Ops:
  0.6 86.6 %grouped_attention_backward.1 = (bf16[384,3584]{1,0:T(8,128)(2,1)}, bf16[384,1792]{1,0:T(8,128)(2,1)}, f32[224,512]{1,0:T(8,128)}) custom-call(s32[1,6]{1,0:T(1,128)} %ids_ref.1, s32[1,6]{1,0:T(1,128)} %flags_ref.1, bf16[224,512]{1,0:T(8,128)(2,1)} %w_ref.1, f32[1,128]{1,0:T(1,128)} %constant.2.clone.freq_ref, bf16[384,3584]{1,0:T(8,128)(2,1)} %x_hbm.1, ...), custom_call_target="tpu_custom_call" | custom-call | tf_op jit(solution)/shard_map/grouped_attention_backward/pallas_call | solution.py:549
  87.2 140.2 %write_results.1 = (bf16[384,3584]{1,0:T(8,128)(2,1)}, bf16[384,1792]{1,0:T(8,128)(2,1)}, f32[224,512]{1,0:T(8,128)}) custom-call(bf16[384,3584]{1,0:T(8,128)(2,1)} %get-tuple-element.6.refs_0_, bf16[384,1792]{1,0:T(8,128)(2,1)} %get-tuple-element.7.refs_1_, f32[224,512]{1,0:T(8,128)} %get-tuple-element.8.refs_2_), custom_call_target="tpu_custom_call" | custom-call | tf_op jit(solution)/shard_map/write_results/pallas_call | solution.py:621

commit v4 on v3

--- a/solution.py
+++ b/solution.py
@@ -66,18 +66,19 @@
 
 
 HOPS = {1: 4, -1: 3}
+LATE = 9
 ARRIVES = {1: 2, 2: 1, 3: 3, 4: 4}
 WAYS = [(1, 1), (-1, 1), (1, 2), (-1, 2), (1, 3), (-1, 3), (1, 4)]
 
 
 def kernel(
     ids_ref, flags_ref, w_ref, freq_ref, x_hbm, q_hbm, g_hbm,
-    gi_hbm, gq_hbm, gw_hbm,
+    gi, gq, gw,
     x_ref, q_ref, g_ref, x_t, weight,
     keys, keys_t, vals, kacc, vacc, bias, cosine, sine, to_pack, from_pack, kept,
-    qg, qp, qr, kvg, kvp, kvr, chosen, gi, gq, gw,
+    held, qg, qp, qr, kvg, kvp, kvr, chosen,
     part, sib, tot, relay_in, relay_out, direct, summed, after_x, z_in, after_z, y_in, final, shared,
-    load, store, g_send, ring_recv, gy_recv, gx_recv, near_recv, far_recv,
+    load, g_send, ring_recv, gy_recv, gx_recv, near_recv, far_recv,
     q_send, q_recv, kv_send, kv_recv,
     d_send, sib_recv, relay_recv, direct_recv, summed_recv, z_recv, y_recv, share_send, share_recv,
 ):
@@ -201,8 +202,6 @@
 
     pieces = {1: piece_1, 2: piece_2, 3: piece_3, 4: piece_4}
 
-    near = 2 * (x % 2) + c
-    far = 2 * (1 - x % 2) + c
     push, gather_started = pusher(g_send)
 
     def source(way, hop):
@@ -211,77 +210,94 @@
     def slot(way, hop):
         return 7 if hop == 0 else WAYS.index((way, hop))
 
-    def from_ring(way, hop):
-        part = weight.at[near, hi, source(way, hop)]
+    def piece(p, kind, row, zs, core):
+        rows = pl.ds(pl.multiple_of(core * HALF, HALF), HALF)
+        return weight.at[KVH * kind + p, row, zs, rows]
+
+    near, far = x % 2, 1 - x % 2
+
+    def gather_start(p):
+        own = piece(p, near, hi, z, c)
+        push(own, own, z_peer[1], ring_recv.at[p * 8 + slot(1, 2)])
+        push(own, own, z_peer[5], ring_recv.at[p * 8 + slot(-1, 2)])
+        push(own, own, z_peer[0], ring_recv.at[p * 8 + slot(1, 1)])
+        push(own, own, z_peer[6], ring_recv.at[p * 8 + slot(-1, 1)])
+        push(own, own, cross, gy_recv.at[p * 8 + slot(1, 0)])
+
+    def from_ring(p, way, hop):
+        part = piece(p, near, hi, source(way, hop), c)
         at = slot(way, hop)
-        arrived(part, ring_recv.at[at])
+        arrived(part, ring_recv.at[p * 8 + at])
         if hop == 2:
-            push(part, part, z_peer[0 if way == 1 else 6], ring_recv.at[slot(way, 3)])
+            push(part, part, z_peer[0 if way == 1 else 6], ring_recv.at[p * 8 + slot(way, 3)])
             if way == 1:
-                push(part, part, z_peer[1], ring_recv.at[slot(way, 4)])
-        push(part, part, cross, gy_recv.at[at])
-        push(part, part, x_peer[0 if way == 1 else 1], gx_recv.at[at])
-        push(part, part, sibling, near_recv.at[at])
-
-    def from_y(way, hop):
-        part = weight.at[near, oth, source(way, hop)]
+                push(part, part, z_peer[1], ring_recv.at[p * 8 + slot(way, 4)])
+        push(part, part, cross, gy_recv.at[p * 8 + at])
+        push(part, part, x_peer[0 if way == 1 else 1], gx_recv.at[p * 16 + at])
+        push(part, part, sibling, near_recv.at[p * 16 + at])
+
+    def from_y(p, way, hop):
+        part = piece(p, near, oth, source(way, hop), c)
         at = slot(way, hop)
-        arrived(part, gy_recv.at[at])
-        push(part, part, x_peer[1 if way == 1 and hop else 0], gx_recv.at[8 + at])
-        push(part, part, sibling, near_recv.at[8 + at])
-
-    def from_x(row, half, way, hop):
-        part = weight.at[far, row, source(way, hop)]
-        at = half * 8 + slot(way, hop)
+        arrived(part, gy_recv.at[p * 8 + at])
+        push(part, part, x_peer[1 if way == 1 and hop else 0], gx_recv.at[p * 16 + 8 + at])
+        push(part, part, sibling, near_recv.at[p * 16 + 8 + at])
+
+    def from_x(p, row, half, way, hop):
+        part = piece(p, far, row, source(way, hop), c)
+        at = p * 16 + half * 8 + slot(way, hop)
         arrived(part, gx_recv.at[at])
         push(part, part, sibling, far_recv.at[at])
 
-    own = weight.at[near, hi, z]
-    push(own, own, z_peer[1], ring_recv.at[slot(1, 2)])
-    push(own, own, z_peer[5], ring_recv.at[slot(-1, 2)])
-    push(own, own, z_peer[0], ring_recv.at[slot(1, 1)])
-    push(own, own, z_peer[6], ring_recv.at[slot(-1, 1)])
-    push(own, own, cross, gy_recv.at[slot(1, 0)])
-    piece_0()
-    for time in range(1, 7):
+    def gather_step(p, time):
         for way in (1, -1):
             if time in ARRIVES and ARRIVES[time] <= HOPS[way]:
-                from_ring(way, ARRIVES[time])
+                from_ring(p, way, ARRIVES[time])
         if time == 2:
-            from_y(1, 0)
+            from_y(p, 1, 0)
         for way in (1, -1):
             if time - 1 in ARRIVES and ARRIVES[time - 1] <= HOPS[way]:
-                from_y(way, ARRIVES[time - 1])
+                from_y(p, way, ARRIVES[time - 1])
         if time == 3:
-            from_x(oth, 1, 1, 0)
+            from_x(p, oth, 1, 1, 0)
         for way in (1, -1):
             if time - 1 in ARRIVES and ARRIVES[time - 1] <= HOPS[way]:
-                from_x(hi, 0, way, ARRIVES[time - 1])
+                from_x(p, hi, 0, way, ARRIVES[time - 1])
             if time - 2 in ARRIVES and ARRIVES[time - 2] <= HOPS[way]:
-                from_x(oth, 1, way, ARRIVES[time - 2])
-        if time in pieces:
-            pieces[time]()
-    for half, row in ((0, hi), (1, oth)):
-        for way, hop in WAYS + [(1, 0)] * half:
-            at = half * 8 + slot(way, hop)
-            arrived(weight.at[2 * (x % 2) + 1 - c, row, source(way, hop)], near_recv.at[at])
-            arrived(weight.at[2 * (1 - x % 2) + 1 - c, row, source(way, hop)], far_recv.at[at])
-
-    def weight_rows(n):
+                from_x(p, oth, 1, way, ARRIVES[time - 2])
+
+    def gather_end(p):
+        for half, row in ((0, hi), (1, oth)):
+            for way, hop in WAYS + [(1, 0)] * half:
+                at = p * 16 + half * 8 + slot(way, hop)
+                arrived(piece(p, near, row, source(way, hop), 1 - c), near_recv.at[at])
+                arrived(piece(p, far, row, source(way, hop), 1 - c), far_recv.at[at])
+
+    def weight_rows(n, blocks=range(2 * KVH)):
         at = pl.ds((n % 2) * 4, 4)
-        return jnp.concatenate(
-            [weight[q, n // 2, at].reshape(CHUNK, HD) for q in range(2 * KVH)], axis=1
-        )
-
-    projected = jnp.zeros((ROWS, KV), f32)
-    for n in range(4):
-        projected += dot(x_ref[:, n * CHUNK : (n + 1) * CHUNK], weight_rows(n), (1, 0))
-    for g in range(KVH):
-        raw = projected[:, g * HD : (g + 1) * HD]
+        return jnp.concatenate([weight[q, n // 2, at].reshape(CHUNK, HD) for q in blocks], axis=1)
+
+    def project(g):
+        projected = jnp.zeros((ROWS, 2 * HD), f32)
+        for n in range(4):
+            rows = weight_rows(n, (g, KVH + g))
+            projected += dot(x_ref[:, n * CHUNK : (n + 1) * CHUNK], rows, (1, 0))
+        raw = projected[:, :HD]
         key = raw * cosine[...] + pltpu.roll(raw, HD // 2, 1) * sine[...]
         keys[g] = key.astype(bf16)
         keys_t[g] = key.T.astype(bf16)
-        vals[g] = projected[:, (KVH + g) * HD : (KVH + g + 1) * HD].astype(bf16)
+        vals[g] = projected[:, HD:].astype(bf16)
+
+    gather_start(0)
+    piece_0()
+    for time in range(1, 7):
+        gather_step(0, time)
+        if time == 4:
+            gather_start(1)
+        if time in pieces:
+            pieces[time]()
+    gather_end(0)
+    project(0)
     loads[1].wait()
     loads[2].wait()
 
@@ -290,7 +306,17 @@
     def hand_over(h):
         return remote(qp.at[h], qr.at[h], partner, q_send.at[h], q_recv.at[h])
 
-    def heads(g, first, last, send_now):
+    def query_part(g, h, dscores_b):
+        own = (dot(keys_t[g], dscores_b, (1, 0)) * scale).T.astype(bf16)
+        qg[h] = own
+        qp[h] = dot(to_pack[...], own, (1, 0)).astype(bf16)
+        hand_over(h).start()
+
+    def late_queries(first, last):
+        for h in range(first, last):
+            query_part(1, h, held[h - LATE])
+
+    def heads(g, first, last):
         for h in range(first, last):
             query, grad = q_ref[:, h * HD : (h + 1) * HD], g_ref[:, h * HD : (h + 1) * HD]
             scores = dot(keys[g], query, (1, 1)) * scale + bias[...]
@@ -302,12 +328,10 @@
             dscores_b = (probs * (dprobs - delta)).astype(bf16)
             vacc[...] += dot(probs_b, grad, (1, 0))
             kacc[...] += dot(dscores_b, query, (1, 0))
-            query_grad = dot(keys_t[g], dscores_b, (1, 0)) * scale
-            own = query_grad.T.astype(bf16)
-            qg[h] = own
-            qp[h] = dot(to_pack[...], own, (1, 0)).astype(bf16)
-            if send_now:
-                hand_over(h).start()
+            if h < LATE:
+                query_part(g, h, dscores_b)
+            else:
+                held[h - LATE] = dscores_b
 
     def clear():
         kacc[...] = jnp.zeros_like(kacc)
@@ -432,13 +456,6 @@
                     shared[g, half, core].astype(f32)
                 )
 
-    stores = []
-
-    def put(src, dst):
-        copy = pltpu.make_async_copy(src, dst, store.at[len(stores)])
-        copy.start()
-        stores.append(copy)
-
     def pick(own, other):
         taken = dot(from_pack[...], other, (1, 0))
         return jnp.where(kept[...] > 0.5, own.astype(f32), taken).astype(bf16)
@@ -453,7 +470,6 @@
         for n in range(4):
             cols = slice(n * CHUNK, (n + 1) * CHUNK)
             gi[:, cols] = dot(chosen[...], weight_rows(n), (1, 1)).astype(bf16)
-            put(gi.at[:, cols], gi_hbm.at[:, cols])
 
     def place_queries(first, last):
         @pl.loop(first, last)
@@ -461,22 +477,22 @@
             arrived(qr.at[h], q_recv.at[h])
             gq[:, columns(h)] = pick(qg[h], qr[h])
 
-        cols = slice(first * HD, last * HD)
-        put(gq.at[:, cols], gq_hbm.at[:, cols])
-
     clear()
-    heads(0, 0, 7, True)
+    for h in range(GROUP):
+        heads(0, h, h + 1)
+        if h < 6:
+            gather_step(1, h + 1)
     finish_group(0)
     clear()
     for i in range(4):
         product(0, i)
-    heads(1, 7, 8, True)
+    gather_end(1)
+    project(1)
     for i in range(4):
         core_sum(0, i)
-    heads(1, 8, 9, True)
-    heads(1, 9, 12, False)
+    heads(1, 7, 11)
     relay(0)
-    heads(1, 12, 14, False)
+    heads(1, 11, 14)
     finish_group(1)
     product(1, 0)
     product(1, 1)
@@ -486,21 +502,20 @@
     product(1, 3)
     core_sum(1, 2)
     core_sum(1, 3)
-    for h in range(9, 14):
-        hand_over(h).start()
     x_sum(0)
+    late_queries(9, 12)
     relay(1)
     z_sum(0)
+    late_queries(12, 14)
     x_sum(1)
+    y_sum(0)
     input_grad()
-    y_sum(0)
     z_sum(1)
     place_queries(0, 7)
     y_sum(1)
     collect(0)
     place_queries(7, 14)
     collect(1)
-    put(gw, gw_hbm)
     for copy in gather_started + d_started:
         copy.wait_send()
     for h in range(QH):
@@ -513,22 +528,6 @@
             for copy in share(g):
                 copy.wait_send()
 
-    for copy in stores:
-        copy.wait()
-
-
-def write_kernel(*refs):
-    sems, copies = refs[6], []
-    for src, dst, parts in zip(refs[:3], refs[3:6], (6, 3, 2)):
-        rows = src.shape[0] // parts
-        for n in range(parts):
-            at = pl.ds(n * rows, rows)
-            copies.append(pltpu.make_async_copy(src.at[at], dst.at[at], sems.at[len(copies)]))
-    for copy in copies:
-        copy.start()
-    for copy in copies:
-        copy.wait()
-
 
 def shards(inputs, queries, out_grad, kv_weight, passage_blocks, handover):
     freq = ROPE_BASE ** (-(np.arange(HD // 2, dtype=np.float32) * 2.0) / HD)
@@ -546,12 +545,12 @@
         jax.ShapeDtypeStruct((ROWS, QH * HD), bf16),
         jax.ShapeDtypeStruct((SHARD, KV), f32),
     )
-    results = pl.pallas_call(
+    return pl.pallas_call(
         kernel,
         name="grouped_attention_backward",
-        out_shape=shapes,
+        out_shape=tuple(pltpu.VMEM(shape.shape, shape.dtype) for shape in shapes),
         in_specs=[scalars, scalars, VMEM, VMEM, anywhere, anywhere, anywhere],
-        out_specs=(anywhere, anywhere, anywhere),
+        out_specs=(VMEM, VMEM, VMEM),
         scratch_shapes=[
             vmem(ROWS, D),
             vmem(ROWS, QH * HD),
@@ -569,6 +568,7 @@
             vmem(packed, ROWS),
             vmem(ROWS, packed),
             vmem(ROWS, HD, kind=f32),
+            vmem(QH - LATE, ROWS, ROWS),
             vmem(QH, ROWS, HD),
             vmem(QH, packed, HD),
             vmem(QH, packed, HD),
@@ -576,9 +576,6 @@
             vmem(KVH, 2, packed, HD),
             vmem(KVH, 2, packed, HD),
             vmem(ROWS, KV),
-            vmem(ROWS, D),
-            vmem(ROWS, QH * HD),
-            vmem(SHARD, KV, kind=f32),
             vmem(KVH, 2, NF, SHARD, HD),
             vmem(KVH, NF, SHARD, HD),
             vmem(KVH, NF, SHARD, HD),
@@ -593,13 +590,12 @@
             vmem(KVH, HALF, HD),
             vmem(KVH, 2, 2, HALF, HD),
             dma((3,)),
-            dma((8,)),
-            dma((64,)),
-            dma((8,)),
-            dma((8,)),
+            dma((128,)),
             dma((16,)),
             dma((16,)),
-            dma((16,)),
+            dma((32,)),
+            dma((32,)),
+            dma((32,)),
             dma((QH,)),
             dma((QH,)),
             dma((KVH,)),
@@ -618,14 +614,7 @@
             collective_id=0, has_side_effects=True, vmem_limit_bytes=LIMIT
         ),
     )(passage_blocks, handover, kv_weight, freq, inputs, queries, out_grad)
-    return pl.pallas_call(
-        write_kernel,
-        name="write_results",
-        out_shape=shapes,
-        in_specs=[anywhere] * 3,
-        out_specs=(anywhere,) * 3,
-        scratch_shapes=[dma((16,))],
-    )(*results)
+
 
 def solution(mesh):
     rows = P(("dp", "fsdp"), None)

time: 228 us -> 99.1 us (0.43)
  Pallas kernels: 227 us -> 95 us
  local copies, waits for them, and re-layouts: 0 us -> 3.38 us
    pallas_call x2 -> x1, Pallas kernels: 227 us -> 95 us  [shards(): pl.pallas_call(kernel, name='grouped_attention_backward', out_shape=tuple...]
    unnamed x0 -> x3, local copies, waits for them, and re-layouts: none -> 3.38 us
where the time goes in v4:
time: 99.1 us; the launch traced here: 99 us
  Pallas kernels  95 us (96%)
  local copies, waits for them, and re-layouts  3.38 us (3%)
    pallas_call x1, Pallas kernels, shards(): pl.pallas_call(kernel, name='grouped_attention_backward', out_shape=tuple...  95 us
    unnamed x3, local copies, waits for them, and re-layouts  3.38 us

profile of v4, /device:TPU:1, one launch (start us, length us, event | category | flops | bytes accessed | tf_op | source)
XLA Modules:
  0.0 99.0 jit_solution(6340518314769074077)
XLA Ops:
  0.6 95.0 %grouped_attention_backward.1 = (bf16[384,3584]{1,0:T(8,128)(2,1)S(1)}, bf16[384,1792]{1,0:T(8,128)(2,1)S(1)}, f32[224,512]{1,0:T(8,128)S(1)}) custom-call(s32[1,6]{1,0:T(1,128)} %ids_ref.1, s32[1,6]{1,0:T(1,128)} %flags_ref.1, bf16[224,512]{1,0:T(8,128)(2,1)} %w_ref.1, f32[1,128]{1,0:T(1,128)} %constant.2.clone.freq_ref, bf16[384,3584]{1,0:T(8,128)(2,1)} %x_hbm.1, ...), custom_call_target="tpu_custom_call" | custom-call | tf_op jit(solution)/shard_map/grouped_attention_backward/pallas_call | solution.py:548
  95.7 1.5 %copy.13 = bf16[384,3584]{1,0:T(8,128)(2,1)} copy(bf16[384,3584]{1,0:T(8,128)(2,1)S(1)} %get-tuple-element.3) | data formatting | bytes 5505024
  97.2 0.8 copy.15
  98.0 1.1 %copy.14 = bf16[384,1792]{1,0:T(8,128)(2,1)} copy(bf16[384,1792]{1,0:T(8,128)(2,1)S(1)} %get-tuple-element.4) | data formatting | bytes 2752512

commit v5 on v4

--- a/solution.py
+++ b/solution.py
@@ -292,12 +292,14 @@
     piece_0()
     for time in range(1, 7):
         gather_step(0, time)
-        if time == 4:
+        if time == 2:
             gather_start(1)
         if time in pieces:
             pieces[time]()
+    gather_step(1, 1)
     gather_end(0)
     project(0)
+    gather_step(1, 2)
     loads[1].wait()
     loads[2].wait()
 
@@ -480,19 +482,20 @@
     clear()
     for h in range(GROUP):
         heads(0, h, h + 1)
-        if h < 6:
-            gather_step(1, h + 1)
+        if h in (1, 3, 5):
+            gather_step(1, 3 + h // 2)
     finish_group(0)
     clear()
     for i in range(4):
         product(0, i)
+    gather_step(1, 6)
+    for i in range(4):
+        core_sum(0, i)
     gather_end(1)
     project(1)
-    for i in range(4):
-        core_sum(0, i)
-    heads(1, 7, 11)
+    heads(1, 7, 13)
     relay(0)
-    heads(1, 11, 14)
+    heads(1, 13, 14)
     finish_group(1)
     product(1, 0)
     product(1, 1)

time: 99.1 us -> 94.1 us (0.950)
  Pallas kernels: 95 us -> 89.9 us
    pallas_call x1, Pallas kernels: 95 us -> 89.9 us  [shards(): pl.pallas_call(kernel, name='grouped_attention_backward', out_shape=tuple...]
where the time goes in v5:
time: 94.1 us; the launch traced here: 94 us
  Pallas kernels  89.9 us (96%)
  local copies, waits for them, and re-layouts  3.38 us (4%)
    pallas_call x1, Pallas kernels, shards(): pl.pallas_call(kernel, name='grouped_attention_backward', out_shape=tuple...  89.9 us
    unnamed x3, local copies, waits for them, and re-layouts  3.38 us

profile of v5, /device:TPU:1, one launch (start us, length us, event | category | flops | bytes accessed | tf_op | source)
XLA Modules:
  0.0 94.0 jit_solution(6406228084957376178)
XLA Ops:
  0.6 89.9 %grouped_attention_backward.1 = (bf16[384,3584]{1,0:T(8,128)(2,1)S(1)}, bf16[384,1792]{1,0:T(8,128)(2,1)S(1)}, f32[224,512]{1,0:T(8,128)S(1)}) custom-call(s32[1,6]{1,0:T(1,128)} %ids_ref.1, s32[1,6]{1,0:T(1,128)} %flags_ref.1, bf16[224,512]{1,0:T(8,128)(2,1)} %w_ref.1, f32[1,128]{1,0:T(1,128)} %constant.2.clone.freq_ref, bf16[384,3584]{1,0:T(8,128)(2,1)} %x_hbm.1, ...), custom_call_target="tpu_custom_call" | custom-call | tf_op jit(solution)/shard_map/grouped_attention_backward/pallas_call | solution.py:551
  90.6 1.5 %copy.13 = bf16[384,3584]{1,0:T(8,128)(2,1)} copy(bf16[384,3584]{1,0:T(8,128)(2,1)S(1)} %get-tuple-element.3) | data formatting | bytes 5505024
  92.1 0.8 copy.15
  92.9 1.1 %copy.14 = bf16[384,1792]{1,0:T(8,128)(2,1)} copy(bf16[384,1792]{1,0:T(8,128)(2,1)S(1)} %get-tuple-element.4) | data formatting | bytes 2752512

commit v6 on v5

--- a/solution.py
+++ b/solution.py
@@ -21,6 +21,7 @@
 CHUNK = 4 * SHARD
 KV = 2 * KVH * HD
 ROPE_BASE = 1000000.0
+LOG2E = 1.4426950408889634
 MESH = pl.DeviceIdType.MESH
 VMEM = pl.BlockSpec(memory_space=pltpu.VMEM)
 LIMIT = 56 * 1024 * 1024
@@ -66,8 +67,8 @@
 
 
 HOPS = {1: 4, -1: 3}
-LATE = 9
-ARRIVES = {1: 2, 2: 1, 3: 3, 4: 4}
+LATE = 6
+ARRIVES = {1: 1, 2: 2, 3: 3, 4: 4}
 WAYS = [(1, 1), (-1, 1), (1, 2), (-1, 2), (1, 3), (-1, 3), (1, 4)]
 
 
@@ -218,20 +219,16 @@
 
     def gather_start(p):
         own = piece(p, near, hi, z, c)
-        push(own, own, z_peer[1], ring_recv.at[p * 8 + slot(1, 2)])
-        push(own, own, z_peer[5], ring_recv.at[p * 8 + slot(-1, 2)])
-        push(own, own, z_peer[0], ring_recv.at[p * 8 + slot(1, 1)])
-        push(own, own, z_peer[6], ring_recv.at[p * 8 + slot(-1, 1)])
-        push(own, own, cross, gy_recv.at[p * 8 + slot(1, 0)])
+        for way, hop in WAYS:
+            peer = z_peer[(hop if way == 1 else NZ - hop) - 1]
+            push(own, own, peer, ring_recv.at[p * 8 + slot(way, hop)])
+            if (way, hop) == (-1, 1):
+                push(own, own, cross, gy_recv.at[p * 8 + slot(1, 0)])
 
     def from_ring(p, way, hop):
         part = piece(p, near, hi, source(way, hop), c)
         at = slot(way, hop)
         arrived(part, ring_recv.at[p * 8 + at])
-        if hop == 2:
-            push(part, part, z_peer[0 if way == 1 else 6], ring_recv.at[p * 8 + slot(way, 3)])
-            if way == 1:
-                push(part, part, z_peer[1], ring_recv.at[p * 8 + slot(way, 4)])
         push(part, part, cross, gy_recv.at[p * 8 + at])
         push(part, part, x_peer[0 if way == 1 else 1], gx_recv.at[p * 16 + at])
         push(part, part, sibling, near_recv.at[p * 16 + at])
@@ -308,21 +305,21 @@
     def hand_over(h):
         return remote(qp.at[h], qr.at[h], partner, q_send.at[h], q_recv.at[h])
 
-    def query_part(g, h, dscores_b):
-        own = (dot(keys_t[g], dscores_b, (1, 0)) * scale).T.astype(bf16)
+    def query_part(h, dscores_b):
+        own = (dot(keys_t[h // GROUP], dscores_b, (1, 0)) * scale).T.astype(bf16)
         qg[h] = own
         qp[h] = dot(to_pack[...], own, (1, 0)).astype(bf16)
         hand_over(h).start()
 
     def late_queries(first, last):
         for h in range(first, last):
-            query_part(1, h, held[h - LATE])
+            query_part(h, held[h - LATE])
 
     def heads(g, first, last):
         for h in range(first, last):
             query, grad = q_ref[:, h * HD : (h + 1) * HD], g_ref[:, h * HD : (h + 1) * HD]
-            scores = dot(keys[g], query, (1, 1)) * scale + bias[...]
-            weights = jnp.exp(scores - jnp.max(scores, axis=0, keepdims=True))
+            scores = dot(keys[g], query, (1, 1)) * (scale * LOG2E) + bias[...]
+            weights = jnp.exp2(scores - jnp.max(scores, axis=0, keepdims=True))
             probs = weights * (1.0 / jnp.sum(weights, axis=0, keepdims=True))
             probs_b = probs.astype(bf16)
             dprobs = dot(vals[g], grad, (1, 1))
@@ -331,7 +328,7 @@
             vacc[...] += dot(probs_b, grad, (1, 0))
             kacc[...] += dot(dscores_b, query, (1, 0))
             if h < LATE:
-                query_part(g, h, dscores_b)
+                query_part(h, dscores_b)
             else:
                 held[h - LATE] = dscores_b
 
@@ -506,10 +503,10 @@
     core_sum(1, 2)
     core_sum(1, 3)
     x_sum(0)
-    late_queries(9, 12)
+    late_queries(6, 11)
     relay(1)
     z_sum(0)
-    late_queries(12, 14)
+    late_queries(11, 14)
     x_sum(1)
     y_sum(0)
     input_grad()

time: 94.1 us -> 93.1 us (0.989)
    pallas_call x1, Pallas kernels: 89.9 us -> 89 us  [shards(): pl.pallas_call(kernel, name='grouped_attention_backward', out_shape=tuple...]
where the time goes in v6:
time: 93.1 us; the launch traced here: 93 us
  Pallas kernels  89 us (96%)
  local copies, waits for them, and re-layouts  3.38 us (4%)
    pallas_call x1, Pallas kernels, shards(): pl.pallas_call(kernel, name='grouped_attention_backward', out_shape=tuple...  89 us
    unnamed x3, local copies, waits for them, and re-layouts  3.38 us

profile of v6, /device:TPU:1, one launch (start us, length us, event | category | flops | bytes accessed | tf_op | source)
XLA Modules:
  0.0 93.0 jit_solution(13022207852881137019)
XLA Ops:
  0.6 89.0 %grouped_attention_backward.1 = (bf16[384,3584]{1,0:T(8,128)(2,1)S(1)}, bf16[384,1792]{1,0:T(8,128)(2,1)S(1)}, f32[224,512]{1,0:T(8,128)S(1)}) custom-call(s32[1,6]{1,0:T(1,128)} %ids_ref.1, s32[1,6]{1,0:T(1,128)} %flags_ref.1, bf16[224,512]{1,0:T(8,128)(2,1)} %w_ref.1, f32[1,128]{1,0:T(1,128)} %constant.2.clone.freq_ref, bf16[384,3584]{1,0:T(8,128)(2,1)} %x_hbm.1, ...), custom_call_target="tpu_custom_call" | custom-call | tf_op jit(solution)/shard_map/grouped_attention_backward/pallas_call | solution.py:548
  89.6 1.5 %copy.13 = bf16[384,3584]{1,0:T(8,128)(2,1)} copy(bf16[384,3584]{1,0:T(8,128)(2,1)S(1)} %get-tuple-element.3) | data formatting | bytes 5505024
  91.1 0.8 copy.15
  91.9 1.1 %copy.14 = bf16[384,1792]{1,0:T(8,128)(2,1)} copy(bf16[384,1792]{1,0:T(8,128)(2,1)S(1)} %get-tuple-element.4) | data formatting | bytes 2752512

commit v7 on v6

--- a/solution.py
+++ b/solution.py
@@ -306,14 +306,15 @@
         return remote(qp.at[h], qr.at[h], partner, q_send.at[h], q_recv.at[h])
 
     def query_part(h, dscores_b):
-        own = (dot(keys_t[h // GROUP], dscores_b, (1, 0)) * scale).T.astype(bf16)
+        own = (dot(keys_t[h // GROUP], dscores_b, (1, 0)) * scale).astype(bf16).T
         qg[h] = own
         qp[h] = dot(to_pack[...], own, (1, 0)).astype(bf16)
-        hand_over(h).start()
 
     def late_queries(first, last):
         for h in range(first, last):
             query_part(h, held[h - LATE])
+        for h in range(first, last):
+            hand_over(h).start()
 
     def heads(g, first, last):
         for h in range(first, last):
@@ -331,6 +332,8 @@
                 query_part(h, dscores_b)
             else:
                 held[h - LATE] = dscores_b
+        for h in range(first, min(last, LATE)):
+            hand_over(h).start()
 
     def clear():
         kacc[...] = jnp.zeros_like(kacc)
@@ -344,6 +347,8 @@
         raw = grad_k * cosine[...] - pltpu.roll(grad_k, HD // 2, 1) * sine[...]
         kvg[g, 0] = raw.astype(bf16)
         kvg[g, 1] = vacc[...].astype(bf16)
+
+    def send_group(g):
         for t in range(2):
             kvp[g, t] = dot(to_pack[...], kvg[g, t], (1, 0)).astype(bf16)
         hand_over_kv(g).start()
@@ -477,15 +482,16 @@
             gq[:, columns(h)] = pick(qg[h], qr[h])
 
     clear()
-    for h in range(GROUP):
-        heads(0, h, h + 1)
-        if h in (1, 3, 5):
-            gather_step(1, 3 + h // 2)
+    for pair in range(3):
+        heads(0, 2 * pair, 2 * pair + 2)
+        gather_step(1, 3 + pair)
+    heads(0, 6, 7)
     finish_group(0)
     clear()
     for i in range(4):
         product(0, i)
     gather_step(1, 6)
+    send_group(0)
     for i in range(4):
         core_sum(0, i)
     gather_end(1)
@@ -502,8 +508,10 @@
     product(1, 3)
     core_sum(1, 2)
     core_sum(1, 3)
+    send_group(1)
     x_sum(0)
-    late_queries(6, 11)
+    late_queries(6, 8)
+    late_queries(8, 11)
     relay(1)
     z_sum(0)
     late_queries(11, 14)

time: 93.1 us -> 93.2 us (level)
  no operation moved by 1% of the time
where the time goes in v7:
time: 93.2 us; the launch traced here: 93.1 us
  Pallas kernels  89.1 us (96%)
  local copies, waits for them, and re-layouts  3.38 us (4%)
    pallas_call x1, Pallas kernels, shards(): pl.pallas_call(kernel, name='grouped_attention_backward', out_shape=tuple...  89.1 us
    unnamed x3, local copies, waits for them, and re-layouts  3.38 us

profile of v7, /device:TPU:1, one launch (start us, length us, event | category | flops | bytes accessed | tf_op | source)
XLA Modules:
  0.0 93.1 jit_solution(12538901706188125631)
XLA Ops:
  0.6 89.1 %grouped_attention_backward.1 = (bf16[384,3584]{1,0:T(8,128)(2,1)S(1)}, bf16[384,1792]{1,0:T(8,128)(2,1)S(1)}, f32[224,512]{1,0:T(8,128)S(1)}) custom-call(s32[1,6]{1,0:T(1,128)} %ids_ref.1, s32[1,6]{1,0:T(1,128)} %flags_ref.1, bf16[224,512]{1,0:T(8,128)(2,1)} %w_ref.1, f32[1,128]{1,0:T(1,128)} %constant.2.clone.freq_ref, bf16[384,3584]{1,0:T(8,128)(2,1)} %x_hbm.1, ...), custom_call_target="tpu_custom_call" | custom-call | tf_op jit(solution)/shard_map/grouped_attention_backward/pallas_call | solution.py:556
  89.8 1.5 %copy.13 = bf16[384,3584]{1,0:T(8,128)(2,1)} copy(bf16[384,3584]{1,0:T(8,128)(2,1)S(1)} %get-tuple-element.3) | data formatting | bytes 5505024
  91.3 0.8 copy.15
  92.1 1.1 %copy.14 = bf16[384,1792]{1,0:T(8,128)(2,1)} copy(bf16[384,1792]{1,0:T(8,128)(2,1)S(1)} %get-tuple-element.4) | data formatting | bytes 2752512

commit v8 on v6

--- a/solution.py
+++ b/solution.py
@@ -508,9 +508,9 @@
     z_sum(0)
     late_queries(11, 14)
     x_sum(1)
-    y_sum(0)
     input_grad()
     z_sum(1)
+    y_sum(0)
     place_queries(0, 7)
     y_sum(1)
     collect(0)

time: 93.1 us -> 93.1 us (level)
  no operation moved by 1% of the time
where the time goes in v8:
time: 93.1 us; the launch traced here: 93 us
  Pallas kernels  89 us (96%)
  local copies, waits for them, and re-layouts  3.38 us (4%)
    pallas_call x1, Pallas kernels, shards(): pl.pallas_call(kernel, name='grouped_attention_backward', out_shape=tuple...  89 us
    unnamed x3, local copies, waits for them, and re-layouts  3.38 us

profile of v8, /device:TPU:1, one launch (start us, length us, event | category | flops | bytes accessed | tf_op | source)
XLA Modules:
  0.0 93.0 jit_solution(18293254733971903335)
XLA Ops:
  0.6 89.0 %grouped_attention_backward.1 = (bf16[384,3584]{1,0:T(8,128)(2,1)S(1)}, bf16[384,1792]{1,0:T(8,128)(2,1)S(1)}, f32[224,512]{1,0:T(8,128)S(1)}) custom-call(s32[1,6]{1,0:T(1,128)} %ids_ref.1, s32[1,6]{1,0:T(1,128)} %flags_ref.1, bf16[224,512]{1,0:T(8,128)(2,1)} %w_ref.1, f32[1,128]{1,0:T(1,128)} %constant.2.clone.freq_ref, bf16[384,3584]{1,0:T(8,128)(2,1)} %x_hbm.1, ...), custom_call_target="tpu_custom_call" | custom-call | tf_op jit(solution)/shard_map/grouped_attention_backward/pallas_call | solution.py:548
  89.6 1.5 %copy.13 = bf16[384,3584]{1,0:T(8,128)(2,1)} copy(bf16[384,3584]{1,0:T(8,128)(2,1)S(1)} %get-tuple-element.3) | data formatting | bytes 5505024
  91.2 0.8 copy.15
  91.9 1.1 %copy.14 = bf16[384,1792]{1,0:T(8,128)(2,1)} copy(bf16[384,1792]{1,0:T(8,128)(2,1)S(1)} %get-tuple-element.4) | data formatting | bytes 2752512

commit v9 on v6

--- a/solution.py
+++ b/solution.py
@@ -67,7 +67,7 @@
 
 
 HOPS = {1: 4, -1: 3}
-LATE = 6
+LATE = 9
 ARRIVES = {1: 1, 2: 2, 3: 3, 4: 4}
 WAYS = [(1, 1), (-1, 1), (1, 2), (-1, 2), (1, 3), (-1, 3), (1, 4)]
 
@@ -503,10 +503,10 @@
     core_sum(1, 2)
     core_sum(1, 3)
     x_sum(0)
-    late_queries(6, 11)
+    late_queries(9, 12)
     relay(1)
     z_sum(0)
-    late_queries(11, 14)
+    late_queries(12, 14)
     x_sum(1)
     y_sum(0)
     input_grad()

time: 93.1 us -> 93.9 us (level)
  no operation moved by 1% of the time
where the time goes in v9:
time: 93.9 us; the launch traced here: 93.8 us
  Pallas kernels  89.8 us (96%)
  local copies, waits for them, and re-layouts  3.38 us (4%)
    pallas_call x1, Pallas kernels, shards(): pl.pallas_call(kernel, name='grouped_attention_backward', out_shape=tuple...  89.8 us
    unnamed x3, local copies, waits for them, and re-layouts  3.38 us

profile of v9, /device:TPU:1, one launch (start us, length us, event | category | flops | bytes accessed | tf_op | source)
XLA Modules:
  0.0 93.8 jit_solution(7065637777981134501)
XLA Ops:
  0.6 89.8 %grouped_attention_backward.1 = (bf16[384,3584]{1,0:T(8,128)(2,1)S(1)}, bf16[384,1792]{1,0:T(8,128)(2,1)S(1)}, f32[224,512]{1,0:T(8,128)S(1)}) custom-call(s32[1,6]{1,0:T(1,128)} %ids_ref.1, s32[1,6]{1,0:T(1,128)} %flags_ref.1, bf16[224,512]{1,0:T(8,128)(2,1)} %w_ref.1, f32[1,128]{1,0:T(1,128)} %constant.2.clone.freq_ref, bf16[384,3584]{1,0:T(8,128)(2,1)} %x_hbm.1, ...), custom_call_target="tpu_custom_call" | custom-call | tf_op jit(solution)/shard_map/grouped_attention_backward/pallas_call | solution.py:548
  90.4 1.5 %copy.13 = bf16[384,3584]{1,0:T(8,128)(2,1)} copy(bf16[384,3584]{1,0:T(8,128)(2,1)S(1)} %get-tuple-element.3) | data formatting | bytes 5505024
  92.0 0.8 copy.15
  92.7 1.1 %copy.14 = bf16[384,1792]{1,0:T(8,128)(2,1)} copy(bf16[384,1792]{1,0:T(8,128)(2,1)S(1)} %get-tuple-element.4) | data formatting | bytes 2752512
